TPU v7x, 256 devices: a whole 4x4x8 slice. The times are simulated.
256 devices in a mesh: dp: 32 (over y, z), ctx: 8 (over x, core).
Axes of the slice: x: 4, y: 4, z: 8, core: 2. Of those that a mesh axis runs over, the one named last changes fastest.
Arguments:
- long_tokens: bfloat16 [32, 2048, 1024], P('dp', 'ctx'), may hold values from -6 to 6
- short_tokens: bfloat16 [32, 64, 16, 1024], P('dp', 'ctx'), may hold values from -6 to 6
- projection: bfloat16 [1024, 2048], replicated, may hold values from -0.1875 to 0.1875
- time_bias: float32 [4, 16], replicated, may hold values from -4 to 4
- long_length: int32 [32], P('dp'), may hold values from 257 to 2048, as said below
- short_length: int32 [32, 64], P('dp', 'ctx'), may hold values from 1 to 16, as said below
- long_time: int32 [32, 2048], P('dp', 'ctx'), may hold values from 0 to 5093, as said below
- short_time: int32 [32, 64, 16], P('dp', 'ctx'), may hold values from 0 to 1029, as said below
- destination: int32 [32, 64], P('dp', 'ctx'), may hold values from 0 to 255, as said below
- long_cotangent: bfloat16 [32, 2048, 512], P('dp', 'ctx'), may hold values from -6 to 6
- short_cotangent: bfloat16 [32, 64, 16, 512], P('dp', 'ctx'), may hold values from -6 to 6
Outputs:
- long_output: bfloat16 [32, 2048, 512], P('dp', 'ctx')
- short_output: bfloat16 [32, 64, 16, 512], P('dp', 'ctx')
- long_token_grad: bfloat16 [32, 2048, 1024], P('dp', 'ctx')
- short_token_grad: bfloat16 [32, 64, 16, 1024], P('dp', 'ctx')
- projection_grad: float32 [1024, 2048], P('dp', 'ctx')
- bias_grad: float32 [4, 16], replicated
Inputs may be any that keep to these rules, and one draw needn't show every extreme that they name: `long_length`: positions at or past a stream's length are padding. Some split stream is always 2048 long. `short_length`: positions at or past a stream's length are padding. Some bucket is always full. `long_time`: nondecreasing along each stream. `short_time`: nondecreasing along each stream. `destination`: for every ctx index the map of the first step is one to one on the 256 buckets of that ctx index, and the buckets of one device go to different dp indices.
All inputs are finite; a program needn't handle non-finite values.
Results may differ from a plain program's by a relative error of at most 0.025.
Values may be sent and summed in bfloat16 or wider, within the bound.
A program may use at most 128 MiB of HBM per device.

v0:
```python
import jax
import jax.numpy as jnp
from jax import lax
from jax.sharding import PartitionSpec as P

epsilon = 1e-05


def silu_grad(value):
    sigma = jax.nn.sigmoid(value)
    return sigma * (1.0 + value * (1.0 - sigma))


def layer_norm(mixed):
    average = jnp.mean(mixed, axis=-1, keepdims=True)
    centred = mixed - average
    spread = jnp.mean(centred * centred, axis=-1, keepdims=True)
    return centred * lax.rsqrt(spread + epsilon)


def pair_terms(queries, keys, query_time, key_time, query_place, key_place, length, table, scale):
    scores = jnp.einsum("rhd,chd->hrc", queries, keys, preferred_element_type=jnp.float32) * scale
    bucket = jnp.clip(query_time[:, None] - key_time[None, :], 0, table.shape[1] - 1)
    bias = jnp.zeros(scores.shape, jnp.float32)
    for bucket_id in range(table.shape[1]):
        bias = jnp.where((bucket == bucket_id)[None], table[:, bucket_id][:, None, None], bias)
    visible = (
        (key_place[None, :] <= query_place[:, None])
        & (key_place[None, :] < length)
        & (query_place[:, None] < length)
    )
    return (scores + bias, visible, bucket)


def bucket_sums(score_grad, bucket, levels):
    return jnp.stack(
        [
            jnp.sum(jnp.where((bucket == bucket_id)[None], score_grad, 0.0), axis=(1, 2))
            for bucket_id in range(levels)
        ],
        axis=1,
    )


def split_heads(activations, heads):
    rows = activations.shape[0]
    width = activations.shape[1] // 4
    head_dim = width // heads
    gates = activations[:, :width]
    values = activations[:, width : 2 * width].reshape(rows, heads, head_dim)
    queries = activations[:, 2 * width : 3 * width].reshape(rows, heads, head_dim)
    keys = activations[:, 3 * width :].reshape(rows, heads, head_dim)
    return (gates, values, queries, keys)


def norm_backward(mixed, normed, gates, cotangent):
    cot_rows = cotangent.astype(jnp.float32)
    gate_grad = cot_rows * normed
    pullback = jax.vjp(layer_norm, mixed)[1]
    mixed_grad = pullback(cot_rows * gates)[0].astype(jnp.bfloat16)
    return (gate_grad, mixed_grad)


def bucket_forward(tokens, times, length, projection, table):
    rows = tokens.shape[0]
    heads = table.shape[0]
    projected = jnp.dot(tokens, projection, preferred_element_type=jnp.float32)
    activations = jax.nn.silu(projected).astype(jnp.bfloat16)
    gates, values, queries, keys = split_heads(activations, heads)
    scale = queries.shape[2] ** (-0.5)
    places = jnp.arange(rows, dtype=jnp.int32)
    total, visible, bucket = pair_terms(
        queries, keys, times, times, places, places, length, table, scale
    )
    weights_p = jnp.where(visible[None], jax.nn.silu(total), 0.0).astype(jnp.bfloat16)
    mixed = jnp.einsum(
        "hrc,chd->rhd", weights_p, values, preferred_element_type=jnp.float32
    ).reshape(rows, gates.shape[1])
    normed = layer_norm(mixed)
    output = (normed * gates).astype(jnp.bfloat16)
    return (output, (projected, activations, mixed, normed, total, visible, bucket, weights_p))


def bucket_backward(saved, cotangent, table):
    projected, activations, mixed, normed, total, visible, bucket, weights_p = saved
    rows = projected.shape[0]
    heads = table.shape[0]
    gates, values, queries, keys = split_heads(activations, heads)
    scale = queries.shape[2] ** (-0.5)
    gate_grad, mixed_grad = norm_backward(mixed, normed, gates, cotangent)
    mixed_grad = mixed_grad.reshape(queries.shape)
    prob_grad = jnp.einsum("rhd,chd->hrc", mixed_grad, values, preferred_element_type=jnp.float32)
    score_grad = jnp.where(visible[None], prob_grad * silu_grad(total), 0.0)
    score_half = score_grad.astype(jnp.bfloat16)
    query_grad = (
        jnp.einsum("hrc,chd->rhd", score_half, keys, preferred_element_type=jnp.float32) * scale
    )
    key_grad = (
        jnp.einsum("hrc,rhd->chd", score_half, queries, preferred_element_type=jnp.float32) * scale
    )
    value_grad = jnp.einsum(
        "hrc,rhd->chd", weights_p, mixed_grad, preferred_element_type=jnp.float32
    )
    width = gates.shape[1]
    grads = jnp.concatenate(
        [
            gate_grad,
            value_grad.reshape(rows, width),
            query_grad.reshape(rows, width),
            key_grad.reshape(rows, width),
        ],
        axis=1,
    )
    act_grad = (grads * silu_grad(projected)).astype(jnp.bfloat16)
    return (act_grad, bucket_sums(score_grad, bucket, table.shape[1]))


def token_grads(act_grad, projection):
    flat = act_grad.reshape(-1, projection.shape[1])
    result = lax.dot_general(
        flat, projection, (((1,), (1,)), ((), ())), preferred_element_type=jnp.float32
    )
    return result.astype(jnp.bfloat16).reshape(act_grad.shape[:-1] + (projection.shape[0],))


def route(selector, data):
    flat = data.reshape(data.shape[0], -1)
    shape_out = (selector.shape[0],) + data.shape[1:]
    if data.dtype == jnp.int32:
        return jnp.dot(selector, flat)
    moved = jnp.dot(selector.astype(data.dtype), flat, preferred_element_type=jnp.float32)
    return moved.astype(data.dtype).reshape(shape_out)


def per_device(
    long_tokens,
    short_tokens,
    projection,
    time_bias,
    long_length,
    short_length,
    long_time,
    short_time,
    destination,
    long_cotangent,
    short_cotangent,
):
    rows_long = long_tokens.shape[1]
    model = long_tokens.shape[2]
    heads, levels = time_bias.shape
    width = long_cotangent.shape[2]
    head_dim = width // heads
    scale = head_dim ** (-0.5)
    tokens = long_tokens[0]
    projected = jnp.dot(tokens, projection, preferred_element_type=jnp.float32)
    activations = jax.nn.silu(projected).astype(jnp.bfloat16)
    gates, values, queries, keys = split_heads(activations, heads)
    length = long_length[0]
    own_time = long_time[0]
    own_place = lax.axis_index("ctx") * rows_long + jnp.arange(rows_long, dtype=jnp.int32)
    key_rows = lax.all_gather(keys, "ctx", axis=0, tiled=True)
    value_rows = lax.all_gather(values, "ctx", axis=0, tiled=True)
    time_rows = lax.all_gather(own_time, "ctx", axis=0, tiled=True)
    key_place = jnp.arange(key_rows.shape[0], dtype=jnp.int32)
    total, visible, bucket = pair_terms(
        queries, key_rows, own_time, time_rows, own_place, key_place, length, time_bias, scale
    )
    weights_p = jnp.where(visible[None], jax.nn.silu(total), 0.0).astype(jnp.bfloat16)
    mixed = jnp.einsum("hrc,chd->rhd", weights_p, value_rows, preferred_element_type=jnp.float32)
    mixed = mixed.reshape(rows_long, width)
    normed = layer_norm(mixed)
    long_output = (normed * gates).astype(jnp.bfloat16)
    gate_grad, mixed_grad = norm_backward(mixed, normed, gates, long_cotangent[0])
    mixed_grad = mixed_grad.reshape(rows_long, heads, head_dim)
    key_rows = lax.all_gather(keys, "ctx", axis=0, tiled=True)
    value_rows = lax.all_gather(values, "ctx", axis=0, tiled=True)
    time_rows = lax.all_gather(own_time, "ctx", axis=0, tiled=True)
    count = key_rows.shape[0]
    key_place = jnp.arange(count, dtype=jnp.int32)
    total, visible, bucket = pair_terms(
        queries, key_rows, own_time, time_rows, own_place, key_place, length, time_bias, scale
    )
    weights_p = jnp.where(visible[None], jax.nn.silu(total), 0.0).astype(jnp.bfloat16)
    prob_grad = jnp.einsum(
        "rhd,chd->hrc", mixed_grad, value_rows, preferred_element_type=jnp.float32
    )
    score_grad = jnp.where(visible[None], prob_grad * silu_grad(total), 0.0)
    score_half = score_grad.astype(jnp.bfloat16)
    query_grad = (
        jnp.einsum("hrc,chd->rhd", score_half, key_rows, preferred_element_type=jnp.float32) * scale
    )
    key_part = (
        jnp.einsum("hrc,rhd->chd", score_half, queries, preferred_element_type=jnp.float32) * scale
    )
    value_part = jnp.einsum(
        "hrc,rhd->chd", weights_p, mixed_grad, preferred_element_type=jnp.float32
    )
    key_whole = key_part
    value_whole = value_part
    query_grad, key_whole, value_whole, table_long = (
        query_grad,
        key_whole,
        value_whole,
        bucket_sums(score_grad, bucket, levels),
    )
    key_grad, value_grad = (
        lax.psum_scatter(key_whole, "ctx", scatter_dimension=0, tiled=True),
        lax.psum_scatter(value_whole, "ctx", scatter_dimension=0, tiled=True),
    )
    grads = jnp.concatenate(
        [
            gate_grad,
            value_grad.reshape(rows_long, width),
            query_grad.reshape(rows_long, width),
            key_grad.reshape(rows_long, width),
        ],
        axis=1,
    )
    long_act_grad = (grads * silu_grad(projected)).astype(jnp.bfloat16)
    long_token_grad = token_grads(long_act_grad, projection)
    buckets = short_tokens.shape[1]
    peers = lax.axis_size("dp")
    home_tokens = short_tokens[0]
    home_time = short_time[0]
    home_length = short_length[0]
    target = destination[0]
    target_peer = target // buckets
    target_slot = target % buckets
    chooser = (target_peer[None, :] == jnp.arange(peers, dtype=jnp.int32)[:, None]).astype(
        jnp.int32
    )
    present = jnp.sum(chooser, axis=1)
    routing = jnp.stack(
        [jnp.dot(chooser, target_slot), jnp.dot(chooser, home_length), present], axis=1
    )
    slot_ids = jnp.arange(buckets, dtype=jnp.int32)[:, None]
    sent_tokens = route(chooser, home_tokens)
    sent_time = route(chooser, home_time)
    got_tokens, got_time, got_routing = (
        lax.all_to_all(sent_tokens, "dp", split_axis=0, concat_axis=0, tiled=True),
        lax.all_to_all(sent_time, "dp", split_axis=0, concat_axis=0, tiled=True),
        lax.all_to_all(routing, "dp", split_axis=0, concat_axis=0, tiled=True),
    )
    placer = ((got_routing[:, 0][None, :] == slot_ids) & (got_routing[:, 2][None, :] == 1)).astype(
        jnp.int32
    )
    held_tokens = route(placer, got_tokens)
    held_time = route(placer, got_time)
    held_length = jnp.dot(placer, got_routing[:, 1])
    short_output, saved = jax.vmap(bucket_forward, in_axes=(0, 0, 0, None, None))(
        held_tokens, held_time, held_length, projection, time_bias
    )
    short_act_grad, short_table = jax.vmap(bucket_backward, in_axes=(0, 0, None))(
        saved, short_cotangent[0], time_bias
    )
    held_grad = token_grads(short_act_grad, projection)
    returned = lax.all_to_all(
        route(placer.T, held_grad), "dp", split_axis=0, concat_axis=0, tiled=True
    )
    short_token_grad = route(chooser.T, returned)
    all_tokens = jnp.concatenate([tokens, held_tokens.reshape(-1, model)], axis=0)
    all_grads = jnp.concatenate(
        [long_act_grad, short_act_grad.reshape(-1, projection.shape[1])], axis=0
    )
    row_part = lax.psum_scatter(
        lax.dot_general(
            all_tokens, all_grads, (((0,), (0,)), ((), ())), preferred_element_type=jnp.float32
        ).astype(jnp.bfloat16),
        "dp",
        scatter_dimension=0,
        tiled=True,
    )
    projection_grad = lax.psum_scatter(row_part, "ctx", scatter_dimension=1, tiled=True).astype(
        jnp.float32
    )
    bias_grad = lax.psum(table_long + jnp.sum(short_table, axis=0), ("dp", "ctx"))
    return (
        long_output[None],
        short_output[None],
        long_token_grad[None],
        short_token_grad[None],
        projection_grad,
        bias_grad,
    )


def solution(mesh):
    return jax.shard_map(
        per_device,
        mesh=mesh,
        in_specs=(
            P("dp", "ctx", None),
            P("dp", "ctx", None, None),
            P(),
            P(),
            P("dp"),
            P("dp", "ctx"),
            P("dp", "ctx"),
            P("dp", "ctx", None),
            P("dp", "ctx"),
            P("dp", "ctx", None),
            P("dp", "ctx", None, None),
        ),
        out_specs=(
            P("dp", "ctx", None),
            P("dp", "ctx", None, None),
            P("dp", "ctx", None),
            P("dp", "ctx", None, None),
            P("dp", "ctx"),
            P(),
        ),
        check_vma=False,
    )
```

profile of v0, /device:TPU:1, one launch (start us, length us, event | category | flops | bytes accessed | tf_op | source)
XLA Modules:
  0.0 473.1 jit_solution(7874745310523335738)
XLA Ops:
  7.2 5.0 %multiply_convert_fusion = (bf16[256,2048]{1,0:T(8,128)(2,1)S(1)}, f32[256,2048]{1,0:T(8,128)}) fusion(bf16[1024,2048]{1,0:T(8,128)(2,1)} %param.13, bf16[1,256,1024]{2,1,0:T(8,128)(2,1)} %param.11), kind=kOutput, calls=%fused_computation.52 | convolution fusion | flops 1076363264 | bytes 7864320 | tf_op jit(solution)/shard_map/dot_general | solution.py:155
  12.3 0.8 copy.319
  13.1 0.8 copy.226
  14.7 11.9 %all-gather = s32[1,2048]{1,0:T(1,128)S(1)} all-gather(s32[1,256]{1,0:T(1,128)S(1)} %copy-done.33), channel_id=2, replica_groups=mesh['dp'=32,'ctx'=8] {'ctx'}, dimensions={1}, use_global_device_ids=true | all-gather | bytes 9216 | tf_op jit(solution)/shard_map/all_gather | solution.py:163
  26.8 7.7 %fusion.21 = (pred[256,2048]{1,0:T(8,128)(4,1)S(1)}, pred[256,2048]{1,0:T(8,128)(4,1)S(1)}, pred[256,2048]{1,0:T(8,128)(4,1)S(1)}, pred[256,2048]{1,0:T(8,128)(4...) fusion(s32[2048]{0:T(1024)S(1)} %bitcast.295, ...), kind=kLoop, calls=%fused_computation.50 | loop fusion | flops 9437184 | bytes 8397824 | tf_op jit(solution)/shard_map/eq | solution.py:26
  34.6 1.4 fusion.23
  36.0 0.4 slice_reduce_fusion.15
  36.6 8.6 %all-gather.6.cloned.1.call-done = bf16[2048,4,128]{2,0,1:T(8,128)(2,1)} async-done(((bf16[256,4,128]{2,0,1:T(8,128)(2,1)}), bf16[2048,4,128]{2,0,1:T(8,128)(2,1)}) %all-gather.6.cloned.1.call-update) | async-done | bytes 2097168 | tf_op jit(solution)/shard_map/all_gather | solution.py:161
  45.1 18.5 %select_convert_fusion = (bf16[4,256,2048]{2,1,0:T(8,128)(2,1)}, f32[4,256,2048]{2,1,0:T(8,128)}) fusion(pred[256,2048]{1,0:T(8,128)(4,1)} %fusion.23, f32[4]{0:T(128)S(1)} %get-tuple-element.76, pred[256,2048]{1,0:T(8,128)(4,1)S(1)} %get-tuple-element.92, f32[4]{0:T(128)S(1)} %get-tuple-element.77, pred[256,2048]{1,0:T(8,128)(4,1)S(1)} %get-tuple-element.93, ...), kind=kOutput, calls=%fused_computation.21 | convolution fusion | flops 587202560 | bytes 23855360 | tf_op jit(solution)/shard_map/rhd,chd->hrc/dot_general | solution.py:22
  63.8 13.8 %all-gather.4.cloned.1.call-done = bf16[2048,4,128]{0,2,1:T(8,128)(2,1)} async-done(((bf16[256,4,128]{0,2,1:T(8,128)(2,1)}), bf16[2048,4,128]{0,2,1:T(8,128)(2,1)}) %all-gather.4.cloned.1.call-update) | async-done | bytes 2097168 | tf_op jit(solution)/shard_map/all_gather | solution.py:162
  77.7 4.4 fusion.129
  82.4 0.2 multiply_reduce_fusion
  82.7 1.0 fusion.128
  83.7 5.0 %convolution_bitcast_fusion = f32[2048,4,128]{0,2,1:T(8,128)} fusion(bf16[4,256,2048]{2,1,0:T(8,128)(2,1)} %get-tuple-element.129, f32[256,512]{1,0:T(8,128)S(1)} %get-tuple-element.79, f32[256]{0:T(256)S(1)} %negate_multiply_fusion.1), kind=kOutput, calls=%fused_computation.28 | convolution fusion | flops 537133056 | bytes 8913920 | tf_op jit(solution)/shard_map/hrc,rhd->chd/dot_general | solution.py:195
  88.7 0.2 reduce-scatter.7.cloned.1.call-start
  88.9 1.3 copy-done.4
  90.3 27.4 %select_reduce_fusion = (f32[4]{0:T(128)}, f32[4]{0:T(128)}, f32[4]{0:T(128)}, f32[4]{0:T(128)}, f32[4]{0:T(128)}, /*index=5*/f32[4]{0:T(128)}, f32[4]{0:T(128)}...) fusion(pred[256,2048]{1,0:T(8,128)(4,1)} %copy-done.9, ...), kind=kOutput, calls=%fused_computation.4 | convolution fusion | flops 625213440 | bytes 24118528 | tf_op jit(solution)/shard_map/rhd,chd->hrc/dot_general | solution.py:184
  117.7 2.0 copy-done.1
  119.7 2.8 multiply_bitcast_fusion
  122.5 0.6 copy-done.98
  123.6 0.7 copy.178
  124.3 9.6 %all-to-all-start = ((s32[32,1,3]{2,1,0:T(1,128)}), s32[32,1,3]{2,1,0:T(1,128)S(1)}, u32[]{:S(2)}, u32[]{:S(2)}) async-start(s32[32,1,3]{2,1,0:T(1,128)} %copy.178), calls=%async_computation | async-start | bytes 32768 | tf_op jit(solution)/shard_map/all_to_all | solution.py:242
  133.9 0.9 fusion.92
  134.9 7.5 %all-to-all-done = s32[32,1,3]{2,1,0:T(1,128)S(1)} async-done(((s32[32,1,3]{2,1,0:T(1,128)}), s32[32,1,3]{2,1,0:T(1,128)S(1)}, u32[]{:S(2)}, u32[]{:S(2)}) %all-to-all-start) | async-done | bytes 416 | tf_op jit(solution)/shard_map/all_to_all | solution.py:242
  142.5 3.8 all-to-all-start.2
  146.3 0.5 convolution_convert_fusion.1
  146.8 1.6 copy.243
  148.5 6.4 %all-to-all-done.2 = s32[32,1,16]{2,1,0:T(1,128)S(1)} async-done(((s32[32,1,16]{2,1,0:T(1,128)}), s32[32,1,16]{2,1,0:T(1,128)S(1)}, u32[]{:S(2)}, u32[]{:S(2)}) %all-to-all-start.2) | async-done | bytes 2080 | tf_op jit(solution)/shard_map/all_to_all | solution.py:241
  154.9 3.9 all-to-all-start.1
  158.8 0.3 reduce-scatter.9.cloned.1.call-start
  159.6 0.3 fusion.88
  160.0 22.4 %all-to-all-done.1 = bf16[32,16,1024]{2,1,0:T(8,128)(2,1)S(1)} async-done(((bf16[32,16,1024]{2,1,0:T(8,128)(2,1)}), bf16[32,16,1024]{2,1,0:T(8,128)(2,1)S(1)}, u32[]{:S(2)}, u32[]{:S(2)}) %all-to-all-start.1) | async-done | bytes 1048608 | tf_op jit(solution)/shard_map/all_to_all | solution.py:240
  182.4 0.6 copy.244
  183.0 0.2 convolution_convert_fusion.3
  183.5 3.1 multiply_convert_fusion.1
  187.0 0.4 fusion.34
  187.5 0.3 bitcast_reduce_fusion
  188.2 0.2 fusion.110
  188.4 0.9 fusion.52
  189.3 1.0 convolution_bitcast_fusion.1
  190.4 2.1 select_reduce_fusion.16
  192.5 0.2 fusion.32
  193.0 0.4 fusion.35
  193.4 1.5 fusion.28
  194.9 0.2 copy.229
  195.2 1.2 copy.228
  196.5 1.2 copy.230
  197.7 2.4 fusion.2
  200.1 1.0 copy-done.6
  201.0 4.3 convolution_convert_fusion.4
  205.4 0.6 copy-done.48
  206.6 3.7 convolution_convert_fusion.6
  210.7 0.5 convolution_convert_fusion
  211.2 1.9 copy.245
  213.1 7.5 %all-to-all-start.3 = ((bf16[32,16,1024]{2,1,0:T(8,128)(2,1)}), bf16[32,16,1024]{2,1,0:T(8,128)(2,1)S(1)}, u32[]{:S(2)}, u32[]{:S(2)}) async-start(bf16[32,16,1024]{2,1,0:T(8,128)(2,1)} %bitcast.111), calls=%async_computation.5 | async-start | bytes 2097152 | tf_op jit(solution)/shard_map/all_to_all | solution.py:257
  221.9 80.8 %psum.7 = f32[4,16]{0,1:T(8,128)S(1)} all-reduce(f32[4,16]{0,1:T(8,128)S(1)} %add.111), channel_id=1, replica_groups=mesh['dp'=32,'ctx'=8] {'dp','ctx'}, use_global_device_ids=true, to_apply=%region_46.47 | all-reduce | flops 64 | bytes 512 | tf_op jit(solution)/shard_map/psum | solution.py:276
  302.7 0.7 copy.221
  303.3 0.6 copy.246
  303.9 0.3 convolution_convert_fusion.2
  304.2 0.9 copy.220
  305.1 123.4 %reduce-scatter.9.cloned.1.call-done = bf16[32,2048]{1,0:T(8,128)(2,1)} async-done(((bf16[1024,2048]{1,0:T(8,128)(2,1)}), bf16[32,2048]{1,0:T(8,128)(2,1)}) %reduce-scatter.9.cloned.1.call-update) | async-done | bytes 131088 | tf_op jit(solution)/shard_map/reduce_scatter | solution.py:265
  428.5 4.3 fusion.27
  432.8 32.2 %reduce-scatter.11.cloned.1.call-done = bf16[32,256]{1,0:T(8,128)(2,1)} async-done(((bf16[32,2048]{1,0:T(8,128)(2,1)}), bf16[32,256]{1,0:T(8,128)(2,1)}) %reduce-scatter.11.cloned.1.call-update) | async-done | bytes 16400 | tf_op jit(solution)/shard_map/reduce_scatter | solution.py:273
  465.0 1.3 convert_element_type.138
  (278 shorter events, 4.9 us)
Async XLA Ops:
  7.2 126.7 %copy-start = (s32[1,8,16]{2,1,0:T(8,128)S(1)}, s32[1,8,16]{2,1,0:T(8,128)}, u32[]{:S(2)}) copy-start(s32[1,8,16]{2,1,0:T(8,128)} %param.18) | copy-start | bytes 1540
  7.2 38.0 %all-gather.6.cloned.1.call-start = ((), (), s32[]{:S(2)}) async-start(), calls=%async_computation.9 | async-start | bytes 2359296 | tf_op jit(solution)/shard_map/all_gather | solution.py:161
  13.1 64.6 %all-gather.4.cloned.1.call-start = ((), (), s32[]{:S(2)}) async-start(), calls=%async_computation.8 | async-start | bytes 2359296 | tf_op jit(solution)/shard_map/all_gather | solution.py:162
  14.0 181.2 %reduce-scatter.5.cloned.1.call-start = ((), (), s32[]{:S(2)}) async-start(), calls=%async_computation.10 | async-start | bytes 4718592 | tf_op jit(solution)/shard_map/reduce_scatter | solution.py:208
  34.5 29.1 %copy-start.9 = (pred[256,2048]{1,0:T(8,128)(4,1)}, pred[256,2048]{1,0:T(8,128)(4,1)S(1)}, u32[]{:S(2)}) copy-start(pred[256,2048]{1,0:T(8,128)(4,1)S(1)} %get-tuple-element.91) | copy-start | bytes 1572868
  34.5 29.1 %copy-start.10 = (pred[256,2048]{1,0:T(8,128)(4,1)}, pred[256,2048]{1,0:T(8,128)(4,1)S(1)}, u32[]{:S(2)}) copy-start(pred[256,2048]{1,0:T(8,128)(4,1)S(1)} %get-tuple-element.92) | copy-start | bytes 1572868
  34.5 29.1 %copy-start.11 = (pred[256,2048]{1,0:T(8,128)(4,1)}, pred[256,2048]{1,0:T(8,128)(4,1)S(1)}, u32[]{:S(2)}) copy-start(pred[256,2048]{1,0:T(8,128)(4,1)S(1)} %get-tuple-element.93) | copy-start | bytes 1572868
  34.5 29.1 %copy-start.12 = (pred[256,2048]{1,0:T(8,128)(4,1)}, pred[256,2048]{1,0:T(8,128)(4,1)S(1)}, u32[]{:S(2)}) copy-start(pred[256,2048]{1,0:T(8,128)(4,1)S(1)} %get-tuple-element.94) | copy-start | bytes 1572868
  36.4 27.3 %copy-start.51 = (f32[4]{0:T(128)}, f32[4]{0:T(128)S(1)}, u32[]{:S(2)}) copy-start(f32[4]{0:T(128)S(1)} %get-tuple-element.63) | copy-start | bytes 52
  36.4 27.3 %copy-start.53 = (f32[4]{0:T(128)}, f32[4]{0:T(128)S(1)}, u32[]{:S(2)}) copy-start(f32[4]{0:T(128)S(1)} %get-tuple-element.64) | copy-start | bytes 52
  36.5 27.3 %copy-start.55 = (f32[4]{0:T(128)}, f32[4]{0:T(128)S(1)}, u32[]{:S(2)}) copy-start(f32[4]{0:T(128)S(1)} %get-tuple-element.65) | copy-start | bytes 52
  36.5 27.3 %copy-start.57 = (f32[4]{0:T(128)}, f32[4]{0:T(128)S(1)}, u32[]{:S(2)}) copy-start(f32[4]{0:T(128)S(1)} %get-tuple-element.66) | copy-start | bytes 52
  36.5 27.3 %copy-start.59 = (f32[4]{0:T(128)}, f32[4]{0:T(128)S(1)}, u32[]{:S(2)}) copy-start(f32[4]{0:T(128)S(1)} %get-tuple-element.67) | copy-start | bytes 52
  36.5 27.3 %copy-start.61 = (f32[4]{0:T(128)}, f32[4]{0:T(128)S(1)}, u32[]{:S(2)}) copy-start(f32[4]{0:T(128)S(1)} %get-tuple-element.68) | copy-start | bytes 52
  36.5 27.3 %copy-start.63 = (f32[4]{0:T(128)}, f32[4]{0:T(128)S(1)}, u32[]{:S(2)}) copy-start(f32[4]{0:T(128)S(1)} %get-tuple-element.69) | copy-start | bytes 52
  36.5 27.3 %copy-start.65 = (f32[4]{0:T(128)}, f32[4]{0:T(128)S(1)}, u32[]{:S(2)}) copy-start(f32[4]{0:T(128)S(1)} %get-tuple-element.70) | copy-start | bytes 52
  36.5 27.3 %copy-start.67 = (f32[4]{0:T(128)}, f32[4]{0:T(128)S(1)}, u32[]{:S(2)}) copy-start(f32[4]{0:T(128)S(1)} %get-tuple-element.71) | copy-start | bytes 52
  36.5 27.3 %copy-start.69 = (f32[4]{0:T(128)}, f32[4]{0:T(128)S(1)}, u32[]{:S(2)}) copy-start(f32[4]{0:T(128)S(1)} %get-tuple-element.72) | copy-start | bytes 52
  36.5 27.3 %copy-start.71 = (f32[4]{0:T(128)}, f32[4]{0:T(128)S(1)}, u32[]{:S(2)}) copy-start(f32[4]{0:T(128)S(1)} %get-tuple-element.73) | copy-start | bytes 52
  36.5 27.3 %copy-start.73 = (f32[4]{0:T(128)}, f32[4]{0:T(128)S(1)}, u32[]{:S(2)}) copy-start(f32[4]{0:T(128)S(1)} %get-tuple-element.74) | copy-start | bytes 52
  36.6 27.3 %copy-start.75 = (f32[4]{0:T(128)}, f32[4]{0:T(128)S(1)}, u32[]{:S(2)}) copy-start(f32[4]{0:T(128)S(1)} %get-tuple-element.75) | copy-start | bytes 52
  36.6 27.3 %copy-start.77 = (f32[4]{0:T(128)}, f32[4]{0:T(128)S(1)}, u32[]{:S(2)}) copy-start(f32[4]{0:T(128)S(1)} %get-tuple-element.76) | copy-start | bytes 52
  36.6 27.3 %copy-start.79 = (f32[4]{0:T(128)}, f32[4]{0:T(128)S(1)}, u32[]{:S(2)}) copy-start(f32[4]{0:T(128)S(1)} %get-tuple-element.77) | copy-start | bytes 52
  88.7 107.7 %reduce-scatter.7.cloned.1.call-start = ((), (), s32[]{:S(2)}) async-start(), calls=%async_computation.11 | async-start | bytes 4718592 | tf_op jit(solution)/shard_map/reduce_scatter | solution.py:207
  122.5 12.3 %copy-start.14 = (bf16[1,8,16,1024]{3,2,1,0:T(8,128)(2,1)S(1)}, bf16[1,8,16,1024]{3,2,1,0:T(8,128)(2,1)}, u32[]{:S(2)}) copy-start(bf16[1,8,16,1024]{3,2,1,0:T(8,128)(2,1)} %param.12) | copy-start | bytes 786436
  123.1 31.7 %copy-start.49 = (s32[8]{0:T(128)}, s32[8]{0:T(128)S(1)}, u32[]{:S(2)}) copy-start(s32[8]{0:T(128)S(1)} %fusion.116) | copy-start | bytes 100
  124.3 18.1 %all-to-all-start = ((s32[32,1,3]{2,1,0:T(1,128)}), s32[32,1,3]{2,1,0:T(1,128)S(1)}, u32[]{:S(2)}, u32[]{:S(2)}) async-start(s32[32,1,3]{2,1,0:T(1,128)} %copy.178), calls=%async_computation | async-start | bytes 32768 | tf_op jit(solution)/shard_map/all_to_all | solution.py:242
  142.5 12.4 %all-to-all-start.2 = ((s32[32,1,16]{2,1,0:T(1,128)}), s32[32,1,16]{2,1,0:T(1,128)S(1)}, u32[]{:S(2)}, u32[]{:S(2)}) async-start(s32[32,1,16]{2,1,0:T(1,128)} %bitcast.81), calls=%async_computation.2 | async-start | bytes 32768 | tf_op jit(solution)/shard_map/all_to_all | solution.py:241
  154.9 27.5 %all-to-all-start.1 = ((bf16[32,16,1024]{2,1,0:T(8,128)(2,1)}), bf16[32,16,1024]{2,1,0:T(8,128)(2,1)S(1)}, u32[]{:S(2)}, u32[]{:S(2)}) async-start(bf16[32,16,1024]{2,1,0:T(8,128)(2,1)} %bitcast.107), calls=%async_computation.1 | async-start | bytes 2097152 | tf_op jit(solution)/shard_map/all_to_all | solution.py:240
  158.8 269.7 %reduce-scatter.9.cloned.1.call-start = ((), (), s32[]{:S(2)}) async-start(), calls=%async_computation.12 | async-start | bytes 4325376 | tf_op jit(solution)/shard_map/reduce_scatter | solution.py:265
  159.5 28.0 %copy-start.31 = (pred[8,16,16]{2,1,0:T(8,128)(4,1)}, pred[8,16,16]{2,1,0:T(8,128)(4,1)S(1)}, u32[]{:S(2)}) copy-start(pred[8,16,16]{2,1,0:T(8,128)(4,1)S(1)} %and_and_fusion) | copy-start | bytes 6148
  159.9 26.8 %copy-start.15 = (pred[8,16,16]{2,1,0:T(8,128)(4,1)}, pred[8,16,16]{2,1,0:T(8,128)(4,1)S(1)}, u32[]{:S(2)}) copy-start(pred[8,16,16]{2,1,0:T(8,128)(4,1)S(1)} %get-tuple-element.117) | copy-start | bytes 6148
  159.9 26.8 %copy-start.17 = (pred[8,16,16]{2,1,0:T(8,128)(4,1)}, pred[8,16,16]{2,1,0:T(8,128)(4,1)S(1)}, u32[]{:S(2)}) copy-start(pred[8,16,16]{2,1,0:T(8,128)(4,1)S(1)} %get-tuple-element.118) | copy-start | bytes 6148
  159.9 26.8 %copy-start.19 = (pred[8,16,16]{2,1,0:T(8,128)(4,1)}, pred[8,16,16]{2,1,0:T(8,128)(4,1)S(1)}, u32[]{:S(2)}) copy-start(pred[8,16,16]{2,1,0:T(8,128)(4,1)S(1)} %get-tuple-element.119) | copy-start | bytes 6148
  159.9 26.8 %copy-start.21 = (pred[8,16,16]{2,1,0:T(8,128)(4,1)}, pred[8,16,16]{2,1,0:T(8,128)(4,1)S(1)}, u32[]{:S(2)}) copy-start(pred[8,16,16]{2,1,0:T(8,128)(4,1)S(1)} %get-tuple-element.120) | copy-start | bytes 6148
  159.9 26.8 %copy-start.23 = (pred[8,16,16]{2,1,0:T(8,128)(4,1)}, pred[8,16,16]{2,1,0:T(8,128)(4,1)S(1)}, u32[]{:S(2)}) copy-start(pred[8,16,16]{2,1,0:T(8,128)(4,1)S(1)} %get-tuple-element.121) | copy-start | bytes 6148
  159.9 26.8 %copy-start.25 = (pred[8,16,16]{2,1,0:T(8,128)(4,1)}, pred[8,16,16]{2,1,0:T(8,128)(4,1)S(1)}, u32[]{:S(2)}) copy-start(pred[8,16,16]{2,1,0:T(8,128)(4,1)S(1)} %get-tuple-element.122) | copy-start | bytes 6148
  159.9 26.8 %copy-start.27 = (pred[8,16,16]{2,1,0:T(8,128)(4,1)}, pred[8,16,16]{2,1,0:T(8,128)(4,1)S(1)}, u32[]{:S(2)}) copy-start(pred[8,16,16]{2,1,0:T(8,128)(4,1)S(1)} %get-tuple-element.123) | copy-start | bytes 6148
  160.0 26.8 %copy-start.29 = (pred[8,16,16]{2,1,0:T(8,128)(4,1)}, pred[8,16,16]{2,1,0:T(8,128)(4,1)S(1)}, u32[]{:S(2)}) copy-start(pred[8,16,16]{2,1,0:T(8,128)(4,1)S(1)} %get-tuple-element.124) | copy-start | bytes 6148
  210.4 10.6 %copy-start.38 = (f32[8,4]{1,0:T(8,128)S(1)}, f32[8,4]{1,0:T(8,128)}, u32[]{:S(2)}) copy-start(f32[8,4]{1,0:T(8,128)} %get-tuple-element.49) | copy-start | bytes 388
  210.4 10.7 %copy-start.37 = (f32[8,4]{1,0:T(8,128)S(1)}, f32[8,4]{1,0:T(8,128)}, u32[]{:S(2)}) copy-start(f32[8,4]{1,0:T(8,128)} %get-tuple-element.50) | copy-start | bytes 388
  210.4 10.7 %copy-start.36 = (f32[8,4]{1,0:T(8,128)S(1)}, f32[8,4]{1,0:T(8,128)}, u32[]{:S(2)}) copy-start(f32[8,4]{1,0:T(8,128)} %get-tuple-element.51) | copy-start | bytes 388
  210.4 10.8 %copy-start.35 = (f32[8,4]{1,0:T(8,128)S(1)}, f32[8,4]{1,0:T(8,128)}, u32[]{:S(2)}) copy-start(f32[8,4]{1,0:T(8,128)} %get-tuple-element.52) | copy-start | bytes 388
  210.4 10.9 %copy-start.34 = (f32[8,4]{1,0:T(8,128)S(1)}, f32[8,4]{1,0:T(8,128)}, u32[]{:S(2)}) copy-start(f32[8,4]{1,0:T(8,128)} %get-tuple-element.53) | copy-start | bytes 388
  210.4 11.2 %copy-start.81 = (f32[4]{0:T(128)S(1)}, f32[4]{0:T(128)}, u32[]{:S(2)}) copy-start(f32[4]{0:T(128)} %get-tuple-element.30) | copy-start | bytes 52
  210.4 11.2 %copy-start.82 = (f32[4]{0:T(128)S(1)}, f32[4]{0:T(128)}, u32[]{:S(2)}) copy-start(f32[4]{0:T(128)} %get-tuple-element.31) | copy-start | bytes 52
  210.5 11.2 %copy-start.83 = (f32[4]{0:T(128)S(1)}, f32[4]{0:T(128)}, u32[]{:S(2)}) copy-start(f32[4]{0:T(128)} %get-tuple-element.32) | copy-start | bytes 52
  210.5 11.2 %copy-start.84 = (f32[4]{0:T(128)S(1)}, f32[4]{0:T(128)}, u32[]{:S(2)}) copy-start(f32[4]{0:T(128)} %get-tuple-element.33) | copy-start | bytes 52
  210.5 11.2 %copy-start.85 = (f32[4]{0:T(128)S(1)}, f32[4]{0:T(128)}, u32[]{:S(2)}) copy-start(f32[4]{0:T(128)} %get-tuple-element.34) | copy-start | bytes 52
  210.5 11.2 %copy-start.86 = (f32[4]{0:T(128)S(1)}, f32[4]{0:T(128)}, u32[]{:S(2)}) copy-start(f32[4]{0:T(128)} %get-tuple-element.35) | copy-start | bytes 52
  210.5 11.2 %copy-start.87 = (f32[4]{0:T(128)S(1)}, f32[4]{0:T(128)}, u32[]{:S(2)}) copy-start(f32[4]{0:T(128)} %get-tuple-element.36) | copy-start | bytes 52
  210.5 11.2 %copy-start.88 = (f32[4]{0:T(128)S(1)}, f32[4]{0:T(128)}, u32[]{:S(2)}) copy-start(f32[4]{0:T(128)} %get-tuple-element.37) | copy-start | bytes 52
  210.5 11.2 %copy-start.89 = (f32[4]{0:T(128)S(1)}, f32[4]{0:T(128)}, u32[]{:S(2)}) copy-start(f32[4]{0:T(128)} %get-tuple-element.38) | copy-start | bytes 52
  210.5 11.2 %copy-start.90 = (f32[4]{0:T(128)S(1)}, f32[4]{0:T(128)}, u32[]{:S(2)}) copy-start(f32[4]{0:T(128)} %get-tuple-element.39) | copy-start | bytes 52
  210.5 11.2 %copy-start.91 = (f32[4]{0:T(128)S(1)}, f32[4]{0:T(128)}, u32[]{:S(2)}) copy-start(f32[4]{0:T(128)} %get-tuple-element.40) | copy-start | bytes 52
  210.5 11.2 %copy-start.92 = (f32[4]{0:T(128)S(1)}, f32[4]{0:T(128)}, u32[]{:S(2)}) copy-start(f32[4]{0:T(128)} %get-tuple-element.41) | copy-start | bytes 52
  210.6 11.2 %copy-start.93 = (f32[4]{0:T(128)S(1)}, f32[4]{0:T(128)}, u32[]{:S(2)}) copy-start(f32[4]{0:T(128)} %get-tuple-element.42) | copy-start | bytes 52
  210.6 11.2 %copy-start.94 = (f32[4]{0:T(128)S(1)}, f32[4]{0:T(128)}, u32[]{:S(2)}) copy-start(f32[4]{0:T(128)} %get-tuple-element.43) | copy-start | bytes 52
  210.6 11.2 %copy-start.95 = (f32[4]{0:T(128)S(1)}, f32[4]{0:T(128)}, u32[]{:S(2)}) copy-start(f32[4]{0:T(128)} %get-tuple-element.44) | copy-start | bytes 52
  210.6 11.2 %copy-start.96 = (f32[4]{0:T(128)S(1)}, f32[4]{0:T(128)}, u32[]{:S(2)}) copy-start(f32[4]{0:T(128)} %get-tuple-element.45) | copy-start | bytes 52
  210.6 93.3 %copy-start.50 = (s32[8]{0:T(128)S(1)}, s32[8]{0:T(128)}, u32[]{:S(2)}) copy-start(s32[8]{0:T(128)} %copy-done.49) | copy-start | bytes 100
  211.2 217.3 %copy-start.7 = (bf16[256,2048]{1,0:T(8,128)(2,1)S(1)}, bf16[256,2048]{1,0:T(8,128)(2,1)}, u32[]{:S(2)}) copy-start(bf16[256,2048]{1,0:T(8,128)(2,1)} %copy-done.6) | copy-start | bytes 3145732
  213.1 90.2 %all-to-all-start.3 = ((bf16[32,16,1024]{2,1,0:T(8,128)(2,1)}), bf16[32,16,1024]{2,1,0:T(8,128)(2,1)S(1)}, u32[]{:S(2)}, u32[]{:S(2)}) async-start(bf16[32,16,1024]{2,1,0:T(8,128)(2,1)} %bitcast.111), calls=%async_computation.5 | async-start | bytes 2097152 | tf_op jit(solution)/shard_map/all_to_all | solution.py:257
  220.6 244.4 %reduce-scatter.11.cloned.1.call-start = ((), (), s32[]{:S(2)}) async-start(), calls=%async_computation.13 | async-start | bytes 147456 | tf_op jit(solution)/shard_map/reduce_scatter | solution.py:273
  (46 other events, 155.8 us)
Sparse Core Ops, SparseCore 0:
  13.2 31.9 all-gather.5
  47.5 30.0 all-gather.3
  88.8 38.1 reduce-scatter.4
  129.4 39.5 reduce-scatter.6
  205.6 222.8 reduce-scatter.8
  431.0 33.9 reduce-scatter.10
where the time goes:
time: 475 us; the launch traced here: 473 us
  waiting for transfers between devices  214 us (45%)
  blocking collectives  92.6 us (19%)
  matrix products  87.4 us (18%)
  starting transfers between devices  25.5 us (5%)
  local copies, waits for them, and re-layouts  20 us (4%)
  other arithmetic  16.7 us (4%)
  between operations  16.5 us (3%)
    reduce_scatter x1, waiting for transfers between devices, per_device(): lax.psum_scatter(lax.dot_general(all_tokens, all_grads, (((0,), (0,)), ((...  123 us
    psum x1, blocking collectives, per_device(): lax.psum(table_long + jnp.sum(short_table, axis=0), ('dp', 'ctx'))  80.8 us
    reduce_scatter x1, waiting for transfers between devices, per_device(): lax.psum_scatter(row_part, 'ctx', scatter_dimension=1, tiled=True)  32.2 us
    dot_general x1, matrix products, per_device(): jnp.einsum('rhd,chd->hrc', mixed_grad, value_rows, preferred_element_type...  27.4 us
    all_to_all x1, waiting for transfers between devices, per_device(): lax.all_to_all(sent_tokens, 'dp', split_axis=0, concat_axis=0, tiled=True)  22.4 us
    dot_general x2, matrix products, pair_terms(): jnp.einsum('rhd,chd->hrc', queries, keys, preferred_element_type=jnp.floa...  19 us
    all_gather x1, waiting for transfers between devices, per_device(): value_rows = lax.all_gather(values, 'ctx', axis=0, tiled=True)  13.8 us
    unnamed x224, local copies, waits for them, and re-layouts  12.5 us
  transfers between devices with their start and end apart: 10, of which 7 were waited for; matrix products, arithmetic and copies ran while one was open for 19% of the time, Pallas kernels for 0%

commit v1 on v0

v1 whole, which is shorter than its diff:
```python
import functools

import jax
import jax.numpy as jnp
from jax import lax
from jax.experimental import pallas as pl
from jax.experimental.pallas import tpu as pltpu
from jax.sharding import PartitionSpec as P

epsilon = 1e-05
MESH = pl.DeviceIdType.MESH
BF = jnp.bfloat16
F32 = jnp.float32
CHIPS = 4
ROWS = 256
HEAD = 128
LEVELS = 16
SLEN = 16
SHORT = 128
MODEL = 1024
BLOCK = 512
SCALE = HEAD ** (-0.5)
VMEM_LIMIT = 56 * 1024 * 1024


def sigmoid(value):
    return 0.5 * jnp.tanh(0.5 * value) + 0.5


def silu_grad(value):
    sigma = sigmoid(value)
    return sigma * (1.0 + value * (1.0 - sigma))


def dot_nn(a, b):
    return jnp.dot(a, b, preferred_element_type=F32)


def dot_nt(a, b):
    return lax.dot_general(a, b, (((1,), (1,)), ((), ())), preferred_element_type=F32)


def dot_tn(a, b):
    return lax.dot_general(a, b, (((0,), (0,)), ((), ())), preferred_element_type=F32)


def column_of(row):
    return jnp.transpose(jnp.broadcast_to(row, (128, 128)))


def iota(shape, axis):
    return lax.broadcasted_iota(jnp.int32, shape, axis)


def remote(src, dst, send_sem, recv_sem, dp, ctx):
    return pltpu.make_async_remote_copy(
        src_ref=src,
        dst_ref=dst,
        send_sem=send_sem,
        recv_sem=recv_sem,
        device_id=(dp, ctx),
        device_id_type=MESH,
    )


def place():
    dp = lax.axis_index("dp")
    ctx = lax.axis_index("ctx")
    return dp, ctx, lax.div(ctx, 2), lax.rem(ctx, 2)


def greet(dp, ctx, n_dp):
    barrier = pltpu.get_barrier_semaphore()

    def to_dp(o, carry):
        pl.semaphore_signal(
            barrier, inc=1, device_id=(lax.rem(dp + o, n_dp), ctx), device_id_type=MESH
        )
        return carry

    lax.fori_loop(1, n_dp, to_dp, 0)

    def to_ctx(o, carry):
        pl.semaphore_signal(
            barrier, inc=1, device_id=(dp, lax.rem(ctx + o, 2 * CHIPS)), device_id_type=MESH
        )
        return carry

    lax.fori_loop(1, 2 * CHIPS, to_ctx, 0)
    pl.semaphore_wait(barrier, n_dp - 1 + 2 * CHIPS - 1)


def lookup(table, diff):
    index = jnp.clip(diff, 0.0, LEVELS - 1.0).astype(jnp.int32)
    parts = [
        jnp.take_along_axis(table, index[:, i : i + 128], axis=1)
        for i in range(0, index.shape[1], 128)
    ]
    return parts[0] if len(parts) == 1 else jnp.concatenate(parts, axis=1)


def gather_kernel(
    n_dp,
    tok,
    w,
    lcot,
    meta,
    scot,
    tok_g,
    p_g,
    act_g,
    kv,
    c_g,
    times,
    c_home,
    place_m,
    wx,
    dtile,
    dest_g,
    cbuf,
    crecv,
    w_sem,
    tok_s,
    tok_r,
    c_s,
    c_r,
    t_s,
    t_r,
    kv_s,
    kv_r,
    d_s,
    d_r,
    s_s,
    s_r,
):
    dp, ctx, chip, core = place()
    sib = ctx + 1 - 2 * core
    loads = []
    for k in range(4):
        col = pl.multiple_of(k * BLOCK + chip * HEAD, HEAD)
        load = pltpu.make_async_copy(
            w.at[:, pl.ds(col, HEAD)], wx.at[:, k * HEAD : (k + 1) * HEAD], w_sem.at[k]
        )
        load.start()
        loads.append(load)
    dtile[...] = jnp.broadcast_to(meta[5:6, :], (8, 128))
    greet(dp, ctx, n_dp)

    def tok_copy(d):
        return remote(
            tok,
            tok_g.at[chip],
            tok_s.at[d],
            tok_r.at[d],
            dp,
            2 * lax.rem(chip + d, CHIPS) + core,
        )

    def c_copy(d):
        peer = lax.rem(chip + d, CHIPS)
        return remote(
            lcot.at[:, pl.ds(pl.multiple_of(peer * HEAD, HEAD), HEAD)],
            c_g.at[chip],
            c_s.at[d],
            c_r.at[d],
            dp,
            2 * peer + core,
        )

    def t_copy(o):
        return remote(
            meta, times.at[ctx], t_s.at[o], t_r.at[o], dp, lax.rem(ctx + o, 2 * CHIPS)
        )

    def d_copy(o):
        return remote(dtile, dest_g.at[dp], d_s.at[o], d_r.at[o], lax.rem(dp + o, n_dp), ctx)

    def s_copy(o):
        peer = lax.rem(dp + o, n_dp)
        return remote(cbuf.at[peer], crecv.at[dp], s_s.at[o], s_r.at[o], peer, ctx)

    for d in (1, 3, 2):
        tok_copy(d).start()

    def start_d(o, carry):
        d_copy(o).start()
        return carry

    lax.fori_loop(1, n_dp, start_d, 0)

    def start_t(o, carry):
        t_copy(o).start()
        return carry

    lax.fori_loop(1, 2 * CHIPS, start_t, 0)
    for d in (1, 3, 2):
        c_copy(d).start()
    tok_g[chip] = tok[...]
    c_g[chip] = lcot[:, pl.ds(pl.multiple_of(chip * HEAD, HEAD), HEAD)]
    times[ctx] = meta[...]
    dest_g[dp] = dtile[...]
    for load in loads:
        load.wait()

    def kv_copy(d):
        src = lax.rem(chip + CHIPS - d, CHIPS)
        return remote(
            kv.at[2 * src + core], kv.at[2 * src + core], kv_s.at[d], kv_r.at[d], dp, sib
        )

    def project(step, carry):
        d = step ^ (step >> 1)
        src = lax.rem(chip + CHIPS - d, CHIPS)

        @pl.when(step > 0)
        def _():
            remote(tok, tok_g.at[src], tok_s.at[d], tok_r.at[d], dp, sib).wait_recv()

        projected = dot_nn(tok_g[src], wx[...])
        p_g[src] = projected
        act = (projected * sigmoid(projected)).astype(BF)
        act_g[src] = act
        kv[2 * src + core, :, 0:HEAD] = act[:, 3 * HEAD : 4 * HEAD]
        kv[2 * src + core, :, HEAD : 2 * HEAD] = act[:, HEAD : 2 * HEAD]
        kv_copy(d).start()
        return carry

    project(0, 0)

    def wait_d(o, carry):
        src = lax.rem(dp + n_dp - o, n_dp)
        remote(dtile, dest_g.at[src], d_s.at[o], d_r.at[o], src, ctx).wait_recv()
        return carry

    lax.fori_loop(1, n_dp, wait_d, 0)
    dest = dest_g[...]
    code = jnp.sum(
        jnp.where((dest >> 3) == dp, ((dest & 7) + 1).astype(F32), 0.0), axis=2, keepdims=True
    )
    code = jnp.broadcast_to(code, (n_dp, 8, 128))
    code = jnp.concatenate([code, code], axis=1).reshape(n_dp * SLEN, 128)
    shape = (n_dp * SLEN, 128)
    same = (iota(shape, 0) & 15) == (iota(shape, 1) & 15)
    slot = ((iota(shape, 1) >> 4) + 1).astype(F32)
    placer = jnp.where(same & (code == slot), 1.0, 0.0).astype(BF)
    place_m[...] = placer
    cbuf[...] = dot_nn(placer, scot[...]).astype(BF).reshape(cbuf.shape)

    def start_s(o, carry):
        s_copy(o).start()
        return carry

    lax.fori_loop(1, n_dp, start_s, 0)
    crecv[dp] = cbuf[dp]

    lax.fori_loop(1, CHIPS, project, 0)

    def wait_s(o, carry):
        src = lax.rem(dp + n_dp - o, n_dp)
        remote(cbuf.at[src], crecv.at[src], s_s.at[o], s_r.at[o], src, ctx).wait_recv()
        return carry

    lax.fori_loop(1, n_dp, wait_s, 0)
    owner = column_of((meta[4:5, :] >> 3).astype(F32))
    owner = jnp.concatenate([owner] * (n_dp * SLEN // 128), axis=1)
    shape = (SHORT, n_dp * SLEN)
    same = (iota(shape, 0) & 15) == (iota(shape, 1) & 15)
    chooser = jnp.where(
        same & (owner == (iota(shape, 1) >> 4).astype(F32)), 1.0, 0.0
    ).astype(BF)
    c_home[...] = dot_nn(chooser, crecv[...].reshape(n_dp * SLEN, BLOCK)).astype(BF)

    for d in (1, 3, 2):
        src = lax.rem(chip + CHIPS - d, CHIPS)
        remote(c_g.at[src], c_g.at[src], c_s.at[d], c_r.at[d], dp, sib).wait_recv()
    for d in range(CHIPS):
        src = lax.rem(chip + CHIPS - d, CHIPS)
        other = kv.at[2 * src + 1 - core]
        remote(other, other, kv_s.at[d], kv_r.at[d], dp, sib).wait_recv()

    def wait_t(o, carry):
        src = lax.rem(ctx + 2 * CHIPS - o, 2 * CHIPS)
        remote(meta, times.at[src], t_s.at[o], t_r.at[o], dp, src).wait_recv()
        return carry

    lax.fori_loop(1, 2 * CHIPS, wait_t, 0)

    def ended_t(o, carry):
        t_copy(o).wait_send()
        return carry

    lax.fori_loop(1, 2 * CHIPS, ended_t, 0)
    for d in (1, 3, 2):
        tok_copy(d).wait_send()
        c_copy(d).wait_send()
    for d in range(CHIPS):
        kv_copy(d).wait_send()

    def ended(o, carry):
        d_copy(o).wait_send()
        s_copy(o).wait_send()
        return carry

    lax.fori_loop(1, n_dp, ended, 0)


def short_kernel(
    n_dp, tok, w, cot, meta, table, token_grad, grad_heads, outbuf, bias, p_ref, grad_flat
):
    tokens = tok[...]
    for k in range(4):
        p_ref[:, k * BLOCK : (k + 1) * BLOCK] = dot_nn(tokens, w[:, k * BLOCK : (k + 1) * BLOCK])
    shape = (SHORT, SHORT)
    row = iota(shape, 0)
    col = iota(shape, 1)
    time_row = meta[2:3, :].astype(F32)
    time_col = column_of(time_row)
    length_col = column_of(meta[3:4, :].astype(F32))
    inside = (row & 15).astype(F32) < length_col
    visible = ((row >> 4) == (col >> 4)) & (col <= row) & inside
    diff = time_col - time_row
    acts, weights, slopes, mixes = [], [], [], []
    for h in range(4):
        parts = []
        for k in range(4):
            v = p_ref[:, k * BLOCK + h * HEAD : k * BLOCK + (h + 1) * HEAD]
            parts.append((v * sigmoid(v)).astype(BF))
        acts.append(parts)
        gates, values, queries, keys = parts
        tab = jnp.broadcast_to(table[h : h + 1, :], shape)
        total = dot_nt(queries, keys) * SCALE + lookup(tab, diff)
        sg = sigmoid(total)
        weight = total * sg
        weights.append(jnp.where(visible, weight, 0.0).astype(BF))
        slopes.append(jnp.where(visible, sg + weight * (1.0 - sg), 0.0))
        mixes.append(dot_nn(weights[h], values))
    mean = sum(jnp.sum(m, axis=1, keepdims=True) for m in mixes) / BLOCK
    centred = [m - mean for m in mixes]
    spread = sum(jnp.sum(m * m, axis=1, keepdims=True) for m in centred) / BLOCK
    scale = lax.rsqrt(spread + epsilon)
    normed = [m * scale for m in centred]
    cots = [cot[:, h * HEAD : (h + 1) * HEAD].astype(F32) for h in range(4)]
    qs = [cots[h] * acts[h][0].astype(F32) for h in range(4)]
    mean_q = sum(jnp.sum(q, axis=1, keepdims=True) for q in qs) / BLOCK
    mean_qn = sum(jnp.sum(q * n, axis=1, keepdims=True) for q, n in zip(qs, normed)) / BLOCK

    bucket = jnp.clip(diff, 0.0, LEVELS - 1.0).astype(jnp.int32)
    level = iota((LEVELS, 128), 0)
    lane = iota((LEVELS, 128), 1)
    sums = jnp.zeros((LEVELS, 128), F32)
    outs = []
    for h in range(4):
        gates, values, queries, keys = acts[h]
        outs.append((normed[h] * gates.astype(F32)).astype(BF))
        mixed_grad = ((qs[h] - mean_q - normed[h] * mean_qn) * scale).astype(BF)
        grad = dot_nt(mixed_grad, values) * slopes[h]
        rows = [
            jnp.sum(jnp.where(bucket == b, grad, 0.0), axis=0, keepdims=True)
            for b in range(LEVELS)
        ]
        per_level = jnp.sum(jnp.concatenate(rows, axis=0), axis=1, keepdims=True)
        sums = sums + jnp.where(lane == h, per_level, 0.0)
        half = grad.astype(BF)
        grads = [
            cots[h] * normed[h],
            dot_tn(weights[h], mixed_grad),
            dot_nn(half, keys) * SCALE,
            dot_tn(half, queries) * SCALE,
        ]
        for k in range(4):
            v = p_ref[:, k * BLOCK + h * HEAD : k * BLOCK + (h + 1) * HEAD]
            g = (grads[k] * silu_grad(v)).astype(BF)
            grad_heads[h, :, k * HEAD : (k + 1) * HEAD] = g
            grad_flat[:, k * BLOCK + h * HEAD : k * BLOCK + (h + 1) * HEAD] = g
    bias[...] = sums
    out = jnp.concatenate(outs, axis=1)
    shape = (n_dp * SLEN, SHORT)
    same = (iota(shape, 0) & 15) == (iota(shape, 1) & 15)
    target = (meta[4:5, :] >> 3).astype(F32)
    sender = jnp.where(same & (target == (iota(shape, 0) >> 4).astype(F32)), 1.0, 0.0).astype(BF)
    outbuf[...] = dot_nn(sender, out).astype(BF).reshape(outbuf.shape)
    flat = grad_flat[...]
    for i in range(0, MODEL, 256):
        token_grad[:, i : i + 256] = dot_nt(flat, w[i : i + 256, :]).astype(BF)


def attend_kernel(
    n_dp,
    act,
    p_g,
    kv,
    cot,
    times,
    table,
    stok,
    sgrad,
    outbuf,
    place_m,
    sbias,
    grad,
    out,
    bias,
    stok_g,
    sgrad_g,
    short_out,
    orecv,
    weight_s,
    slope_s,
    mixed_s,
    hot_s,
    tcol_s,
    trow_s,
    stat_s,
    dk_s,
    dv_s,
    dq_s,
    hist_s,
    tot_s,
    sib_send,
    sib_recv,
    st_s,
    st_r,
    sg_s,
    sg_r,
    o_s,
    o_r,
    stat_sem_s,
    stat_sem_r,
    sib_s,
    sib_r,
):
    dp, ctx, chip, core = place()
    sib = ctx + 1 - 2 * core
    greet(dp, ctx, n_dp)

    def st_copy(d):
        return remote(
            stok, stok_g.at[chip], st_s.at[d], st_r.at[d], dp, 2 * lax.rem(chip + d, CHIPS) + core
        )

    def sg_copy(d):
        peer = lax.rem(chip + d, CHIPS)
        return remote(
            sgrad.at[peer], sgrad_g.at[chip], sg_s.at[d], sg_r.at[d], dp, 2 * peer + core
        )

    def o_copy(o):
        peer = lax.rem(dp + o, n_dp)
        return remote(outbuf.at[peer], orecv.at[dp], o_s.at[o], o_r.at[o], peer, ctx)

    def start_o(o, carry):
        o_copy(o).start()
        return carry

    lax.fori_loop(1, n_dp, start_o, 0)
    for d in (1, 3, 2):
        sg_copy(d).start()
        st_copy(d).start()
    orecv[dp] = outbuf[dp]
    stok_g[chip] = stok[...]
    sgrad_g[chip] = sgrad[chip]

    tab = jnp.broadcast_to(table[pl.ds(chip, 1), :], (ROWS, 128))
    length = times[0, 6:7, 0:1].astype(F32)
    lane = iota((ROWS, 128), 1)

    def times_of(b, carry):
        row = jnp.concatenate([times[b, 0:1, :], times[b, 1:2, :]], axis=1).astype(F32)
        trow_s[b] = jnp.broadcast_to(row, (8, ROWS))
        col = jnp.concatenate([column_of(row[:, 0:128]), column_of(row[:, 128:256])], axis=0)
        tcol_s[b] = col
        hot_s[b] = jnp.where((col.astype(jnp.int32) & 15) == lane, 1.0, 0.0).astype(BF)
        return carry

    lax.fori_loop(0, 2 * CHIPS, times_of, 0)
    dk_s[...] = jnp.zeros_like(dk_s)
    dv_s[...] = jnp.zeros_like(dv_s)
    hist_s[...] = jnp.zeros_like(hist_s)
    tot_s[...] = jnp.zeros_like(tot_s)

    def stat_copy(qs, d):
        return remote(
            stat_s.at[qs, chip],
            stat_s.at[qs, chip],
            stat_sem_s.at[qs, d],
            stat_sem_r.at[qs, d],
            dp,
            2 * lax.rem(chip + d, CHIPS) + core,
        )

    def forward(step, carry):
        qs = CHIPS - 1 - step
        block = 2 * qs + core
        queries = act[qs, :, 2 * HEAD : 3 * HEAD]
        tq = tcol_s[block][:, 0:1]
        spot = iota((ROWS, 1), 0) + block * ROWS
        limit = jnp.where(spot.astype(F32) < length, spot, -1)
        mixed_s[qs] = jnp.zeros((ROWS, HEAD), F32)

        def tile(kb, carry):
            keys = kv[kb, :, 0:HEAD]
            values = kv[kb, :, HEAD : 2 * HEAD]
            tk = trow_s[kb][0:1, :]
            total = dot_nt(queries, keys) * SCALE + lookup(tab, tq - tk)
            sg = sigmoid(total)
            weight = total * sg
            visible = (iota((ROWS, ROWS), 1) + kb * ROWS) <= limit
            weight16 = jnp.where(visible, weight, 0.0).astype(BF)
            weight_s[qs, kb] = weight16
            slope_s[qs, kb] = jnp.where(visible, sg + weight * (1.0 - sg), 0.0)
            mixed_s[qs] += dot_nn(weight16, values)
            return carry

        lax.fori_loop(0, block + 1, tile, 0)
        mixed = mixed_s[qs]
        q = cot[qs].astype(F32) * act[qs, :, 0:HEAD].astype(F32)
        s1 = jnp.sum(mixed, axis=1, keepdims=True)
        centred = mixed - s1 * (1.0 / HEAD)
        s2 = jnp.sum(centred * centred, axis=1, keepdims=True)
        s3 = jnp.sum(q, axis=1, keepdims=True)
        s4 = jnp.sum(q * centred, axis=1, keepdims=True)
        stats = jnp.where(
            lane == 0, s1, jnp.where(lane == 1, s2, jnp.where(lane == 2, s3, s4))
        )
        stat_s[qs, chip] = jnp.transpose(stats)[0:8, :]
        for d in (1, 3, 2):
            stat_copy(qs, d).start()
        return carry

    lax.fori_loop(0, CHIPS, forward, 0)

    def sib_copy(qs):
        return remote(
            sib_send.at[qs], sib_recv.at[qs], sib_s.at[qs], sib_r.at[qs], dp, sib
        )

    def backward(step, carry):
        qs = CHIPS - 1 - step
        block = 2 * qs + core
        for d in (1, 3, 2):
            src = lax.rem(chip + CHIPS - d, CHIPS)
            remote(
                stat_s.at[qs, src],
                stat_s.at[qs, src],
                stat_sem_s.at[qs, d],
                stat_sem_r.at[qs, d],
                dp,
                sib,
            ).wait_recv()
        stats = [stat_s[qs, h] for h in range(4)]
        mean = sum(s[0:1, :] for s in stats) * (1.0 / BLOCK)
        gaps = [s[0:1, :] * (1.0 / HEAD) - mean for s in stats]
        spread = sum(s[1:2, :] + HEAD * g * g for s, g in zip(stats, gaps)) * (1.0 / BLOCK)
        scale = lax.rsqrt(spread + epsilon)
        mean_q = sum(s[2:3, :] for s in stats) * (1.0 / BLOCK)
        mean_qn = sum(s[3:4, :] + g * s[2:3, :] for s, g in zip(stats, gaps))
        mean_qn = mean_qn * scale * (1.0 / BLOCK)
        whole = jnp.concatenate(
            [mean, scale, mean_q, mean_qn, jnp.zeros((124, ROWS), F32)], axis=0
        )
        cols = jnp.transpose(whole)
        mean, scale = cols[:, 0:1], cols[:, 1:2]
        mean_q, mean_qn = cols[:, 2:3], cols[:, 3:4]
        normed = (mixed_s[qs] - mean) * scale
        gates = act[qs, :, 0:HEAD].astype(F32)
        cotangent = cot[qs].astype(F32)
        out[qs] = (normed * gates).astype(BF)
        mixed_grad = ((cotangent * gates - mean_q - normed * mean_qn) * scale).astype(BF)
        grad[qs, :, 0:HEAD] = (cotangent * normed * silu_grad(p_g[qs, :, 0:HEAD])).astype(BF)
        queries = act[qs, :, 2 * HEAD : 3 * HEAD]
        tq = tcol_s[block][:, 0:1]
        dq_s[...] = jnp.zeros_like(dq_s)
        hist_s[0] = jnp.zeros((ROWS, 128), F32)

        def tile(kb, carry):
            keys = kv[kb, :, 0:HEAD]
            values = kv[kb, :, HEAD : 2 * HEAD]
            tk = trow_s[kb][0:1, :]
            score = dot_nt(mixed_grad, values) * slope_s[qs, kb]
            near = jnp.where(tq - tk < LEVELS - 1.0, score, 0.0).astype(BF)
            half = score.astype(BF)
            tot_s[...] += jnp.sum(score.reshape(ROWS // 8, 8, ROWS), axis=0)
            hist_s[0] += dot_nn(near, hot_s[kb])
            dq_s[...] += dot_nn(half, keys)
            dk_s[kb] += dot_tn(half, queries)
            dv_s[kb] += dot_tn(weight_s[qs, kb], mixed_grad)
            return carry

        lax.fori_loop(0, block + 1, tile, 0)
        hist_s[1, 0:128, :] += lax.dot_general(
            hot_s[block].astype(F32),
            hist_s[0],
            (((0,), (0,)), ((), ())),
            precision=lax.Precision.HIGHEST,
            preferred_element_type=F32,
        )
        grad[qs, :, 2 * HEAD : 3 * HEAD] = (
            dq_s[...] * SCALE * silu_grad(p_g[qs, :, 2 * HEAD : 3 * HEAD])
        ).astype(BF)
        other = 2 * qs + 1 - core
        sib_send[qs, :, 0:HEAD] = dk_s[other].astype(BF)
        sib_send[qs, :, HEAD : 2 * HEAD] = dv_s[other].astype(BF)
        sib_copy(qs).start()
        return carry

    lax.fori_loop(0, CHIPS, backward, 0)

    hist = hist_s[1, 0:128, :]
    shape = (128, 128)
    gap = (iota(shape, 0) - iota(shape, 1)) & 15
    rows = [
        jnp.sum(jnp.where(gap == b, hist, 0.0), axis=0, keepdims=True) for b in range(LEVELS - 1)
    ]
    total = jnp.sum(tot_s[...], axis=0, keepdims=True)
    rows.append(total[:, 0:128] + total[:, 128:256] - sum(rows))
    levels = jnp.sum(jnp.concatenate(rows, axis=0), axis=1, keepdims=True)
    bias[...] = sbias[...] + jnp.where(iota((LEVELS, 128), 1) == chip, levels, 0.0)

    def finish(step, carry):
        qs = CHIPS - 1 - step
        sib_copy(qs).wait_recv()
        mine = 2 * qs + core
        dk = (dk_s[mine] + sib_recv[qs, :, 0:HEAD].astype(F32)) * SCALE
        dv = dv_s[mine] + sib_recv[qs, :, HEAD : 2 * HEAD].astype(F32)
        grad[qs, :, HEAD : 2 * HEAD] = (dv * silu_grad(p_g[qs, :, HEAD : 2 * HEAD])).astype(BF)
        grad[qs, :, 3 * HEAD : 4 * HEAD] = (
            dk * silu_grad(p_g[qs, :, 3 * HEAD : 4 * HEAD])
        ).astype(BF)
        return carry

    lax.fori_loop(0, CHIPS, finish, 0)

    def wait_o(o, carry):
        src = lax.rem(dp + n_dp - o, n_dp)
        remote(outbuf.at[src], orecv.at[src], o_s.at[o], o_r.at[o], src, ctx).wait_recv()
        return carry

    lax.fori_loop(1, n_dp, wait_o, 0)
    short_out[...] = dot_tn(
        place_m[...], orecv[...].reshape(n_dp * SLEN, BLOCK)
    ).astype(BF)
    for d in (1, 3, 2):
        src = lax.rem(chip + CHIPS - d, CHIPS)
        remote(stok, stok_g.at[src], st_s.at[d], st_r.at[d], dp, sib).wait_recv()
        remote(sgrad.at[src], sgrad_g.at[src], sg_s.at[d], sg_r.at[d], dp, sib).wait_recv()
        st_copy(d).wait_send()
        sg_copy(d).wait_send()

    def ended_q(qs, carry):
        sib_copy(qs).wait_send()
        for d in (1, 3, 2):
            stat_copy(qs, d).wait_send()
        return carry

    lax.fori_loop(0, CHIPS, ended_q, 0)

    def ended(o, carry):
        o_copy(o).wait_send()
        return carry

    lax.fori_loop(1, n_dp, ended, 0)


def finish_kernel(
    n_dp,
    part,
    grad,
    out,
    tok_g,
    stok_g,
    sgrad_g,
    bias,
    w,
    long_out,
    token_grad,
    proj_grad,
    bias_out,
    wh,
    grad_h,
    half_send,
    half_recv,
    own,
    rs_send,
    rs_recv,
    b_dp,
    b_mid,
    b_ctx,
    piece,
    w_sem,
    g_s,
    g_r,
    l_s,
    l_r,
    p_s,
    p_r,
    rs_s,
    rs_r,
    b1_s,
    b1_r,
    b2_s,
    b2_r,
    f_s,
    f_r,
):
    dp, ctx, chip, core = place()
    sib = ctx + 1 - 2 * core

    def w_copy(h, k):
        return pltpu.make_async_copy(
            w.at[:, k * BLOCK + h * HEAD : k * BLOCK + (h + 1) * HEAD],
            wh.at[h, :, k * HEAD : (k + 1) * HEAD],
            w_sem.at[h, k],
        )

    for h in range(4):
        for k in range(4):
            w_copy(h, k).start()
    greet(dp, ctx, n_dp)

    def g_copy(d):
        peer = lax.rem(chip + d, CHIPS)
        return remote(grad.at[peer], grad_h.at[chip], g_s.at[d], g_r.at[d], dp, 2 * peer + core)

    def l_copy(d):
        peer = lax.rem(chip + d, CHIPS)
        return remote(
            out.at[peer],
            long_out.at[:, pl.ds(pl.multiple_of(chip * HEAD, HEAD), HEAD)],
            l_s.at[d],
            l_r.at[d],
            dp,
            2 * peer + core,
        )

    def b1_copy(o):
        return remote(bias, b_dp.at[dp], b1_s.at[o], b1_r.at[o], lax.rem(dp + o, n_dp), ctx)

    def b2_copy(o):
        return remote(
            b_mid, b_ctx.at[ctx], b2_s.at[o], b2_r.at[o], dp, lax.rem(ctx + o, 2 * CHIPS)
        )

    def rs_copy(o):
        peer = lax.rem(dp + o, n_dp)
        return remote(rs_send.at[peer], rs_recv.at[dp], rs_s.at[o], rs_r.at[o], peer, ctx)

    for d in (1, 3, 2):
        g_copy(d).start()
    for d in (1, 3, 2):
        l_copy(d).start()

    def start_b1(o, carry):
        b1_copy(o).start()
        return carry

    lax.fori_loop(1, n_dp, start_b1, 0)
    b_dp[dp] = bias[...]
    grad_h[chip] = grad[chip]
    long_out[:, pl.ds(pl.multiple_of(chip * HEAD, HEAD), HEAD)] = out[chip]

    def outer(cols, target):
        def one(s, carry):
            a = dot_tn(tok_g[s], grad[s, :, pl.ds(cols, 2 * HEAD)])
            b = dot_tn(stok_g[s], sgrad_g[s, :, pl.ds(cols, 2 * HEAD)])

            @pl.when(s == 0)
            def _():
                target[...] = a + b

            @pl.when(s > 0)
            def _():
                target[...] += a + b

            return carry

        lax.fori_loop(0, CHIPS, one, 0)

    outer(pl.multiple_of((1 - core) * 2 * HEAD, 2 * HEAD), own)
    half_send[...] = own[...].astype(BF)
    pair = remote(half_send, half_recv, p_s, p_r, dp, sib)
    pair.start()
    outer(pl.multiple_of(core * 2 * HEAD, 2 * HEAD), own)
    pair.wait_recv()
    rs_send[...] = (own[...] + half_recv[...].astype(F32)).astype(BF).reshape(rs_send.shape)

    def start_rs(o, carry):
        rs_copy(o).start()
        return carry

    lax.fori_loop(1, n_dp, start_rs, 0)
    rs_recv[dp] = rs_send[dp]

    def wait_b1(o, carry):
        src = lax.rem(dp + n_dp - o, n_dp)
        remote(bias, b_dp.at[src], b1_s.at[o], b1_r.at[o], src, ctx).wait_recv()
        return carry

    lax.fori_loop(1, n_dp, wait_b1, 0)
    b_mid[...] = jnp.sum(b_dp[...], axis=0)

    def start_b2(o, carry):
        b2_copy(o).start()
        return carry

    lax.fori_loop(1, 2 * CHIPS, start_b2, 0)
    b_ctx[ctx] = b_mid[...]

    for h in range(4):
        for k in range(4):
            w_copy(h, k).wait()

    total = jnp.zeros((ROWS, MODEL), F32)
    for d in (0, 1, 3, 2):
        src = lax.rem(chip + CHIPS - d, CHIPS)
        if d:
            remote(grad.at[src], grad_h.at[src], g_s.at[d], g_r.at[d], dp, sib).wait_recv()
        total = total + dot_nt(grad_h[src], wh[src])
    token_grad[...] = total.astype(BF)

    def wait_rs(o, carry):
        src = lax.rem(dp + n_dp - o, n_dp)
        remote(rs_send.at[src], rs_recv.at[src], rs_s.at[o], rs_r.at[o], src, ctx).wait_recv()
        return carry

    lax.fori_loop(1, n_dp, wait_rs, 0)
    piece[...] = jnp.sum(rs_recv[...].astype(F32), axis=0)

    col_out = pl.multiple_of(lax.rem(chip, 2) * HEAD, HEAD)
    mine = lax.rem(chip, 2)

    def f_copy(i):
        target = 2 * (2 * core + i) + lax.div(chip, 2)
        return target, remote(
            piece.at[:, i * HEAD : (i + 1) * HEAD],
            proj_grad.at[:, pl.ds(col_out, HEAD)],
            f_s.at[i],
            f_r.at[mine],
            dp,
            target,
        )

    for i in range(2):
        target, copy = f_copy(i)

        @pl.when(target != ctx)
        def _():
            copy.start()

        @pl.when(target == ctx)
        def _():
            proj_grad[:, pl.ds(col_out, HEAD)] = piece[:, i * HEAD : (i + 1) * HEAD]

    def wait_b2(o, carry):
        src = lax.rem(ctx + 2 * CHIPS - o, 2 * CHIPS)
        remote(b_mid, b_ctx.at[src], b2_s.at[o], b2_r.at[o], dp, src).wait_recv()
        return carry

    lax.fori_loop(1, 2 * CHIPS, wait_b2, 0)
    bias_out[...] = jnp.sum(b_ctx[...], axis=0)
    for d in (1, 3, 2):
        src = lax.rem(chip + CHIPS - d, CHIPS)
        remote(
            out.at[src],
            long_out.at[:, pl.ds(pl.multiple_of(src * HEAD, HEAD), HEAD)],
            l_s.at[d],
            l_r.at[d],
            dp,
            sib,
        ).wait_recv()
    for half in range(2):
        source = 2 * (2 * core + half) + lax.div(chip, 2)

        @pl.when(source != ctx)
        def _():
            remote(
                piece.at[:, 0:HEAD],
                proj_grad.at[:, half * HEAD : (half + 1) * HEAD],
                f_s.at[half],
                f_r.at[half],
                dp,
                source,
            ).wait_recv()

    for i in range(2):
        target, copy = f_copy(i)

        @pl.when(target != ctx)
        def _():
            copy.wait_send()

    for d in (1, 3, 2):
        g_copy(d).wait_send()
        l_copy(d).wait_send()
    pair.wait_send()

    def ended(o, carry):
        rs_copy(o).wait_send()
        b1_copy(o).wait_send()
        return carry

    lax.fori_loop(1, n_dp, ended, 0)

    def ended_b2(o, carry):
        b2_copy(o).wait_send()
        return carry

    lax.fori_loop(1, 2 * CHIPS, ended_b2, 0)


VM = pl.BlockSpec(memory_space=pltpu.VMEM)
ANY = pl.BlockSpec(memory_space=pl.ANY)
DMA = pltpu.SemaphoreType.DMA


def shaped(shape, dtype):
    return jax.ShapeDtypeStruct(shape, dtype)


def params(collective):
    if collective is None:
        return pltpu.CompilerParams(vmem_limit_bytes=VMEM_LIMIT)
    return pltpu.CompilerParams(
        vmem_limit_bytes=VMEM_LIMIT, collective_id=collective, has_side_effects=True
    )


def per_device(
    n_dp,
    long_tokens,
    short_tokens,
    projection,
    time_bias,
    long_length,
    short_length,
    long_time,
    short_time,
    destination,
    long_cotangent,
    short_cotangent,
):
    lanes = jnp.zeros((1, 120), jnp.int32) - 1
    target = destination[0]
    meta = jnp.concatenate(
        [
            long_time.reshape(2, 128),
            short_time.reshape(1, 128),
            jnp.repeat(short_length[0], SLEN)[None],
            jnp.repeat(target, SLEN)[None],
            jnp.concatenate([target[None], lanes], axis=1),
            jnp.broadcast_to(long_length[:, None], (1, 128)),
            jnp.zeros((1, 128), jnp.int32),
        ],
        axis=0,
    )
    table = jnp.pad(time_bias, ((0, 4), (0, 128 - LEVELS)))
    stok = short_tokens.reshape(SHORT, MODEL)
    scot = short_cotangent.reshape(SHORT, BLOCK)

    tok_g, p_g, act, kv, c_g, times, c_home, place_m = pl.pallas_call(
        functools.partial(gather_kernel, n_dp),
        out_shape=(
            shaped((CHIPS, ROWS, MODEL), BF),
            shaped((CHIPS, ROWS, BLOCK), F32),
            shaped((CHIPS, ROWS, BLOCK), BF),
            shaped((2 * CHIPS, ROWS, 2 * HEAD), BF),
            shaped((CHIPS, ROWS, HEAD), BF),
            shaped((2 * CHIPS, 8, 128), jnp.int32),
            shaped((SHORT, BLOCK), BF),
            shaped((n_dp * SLEN, 128), BF),
        ),
        in_specs=[VM, ANY, VM, VM, VM],
        out_specs=(VM,) * 8,
        scratch_shapes=[
            pltpu.VMEM((MODEL, BLOCK), BF),
            pltpu.VMEM((8, 128), jnp.int32),
            pltpu.VMEM((n_dp, 8, 128), jnp.int32),
            pltpu.VMEM((n_dp, SLEN, BLOCK), BF),
            pltpu.VMEM((n_dp, SLEN, BLOCK), BF),
            DMA((4,)),
            DMA((CHIPS,)),
            DMA((CHIPS,)),
            DMA((CHIPS,)),
            DMA((CHIPS,)),
            DMA((2 * CHIPS,)),
            DMA((2 * CHIPS,)),
            DMA((CHIPS,)),
            DMA((CHIPS,)),
            DMA((n_dp,)),
            DMA((n_dp,)),
            DMA((n_dp,)),
            DMA((n_dp,)),
        ],
        compiler_params=params(0),
        name="gather",
    )(long_tokens[0], projection, long_cotangent[0], meta, scot)

    short_grad, grad_heads, outbuf, sbias = pl.pallas_call(
        functools.partial(short_kernel, n_dp),
        out_shape=(
            shaped((SHORT, MODEL), BF),
            shaped((CHIPS, SHORT, BLOCK), BF),
            shaped((n_dp, SLEN, BLOCK), BF),
            shaped((LEVELS, 128), F32),
        ),
        in_specs=[VM] * 5,
        out_specs=(VM,) * 4,
        scratch_shapes=[
            pltpu.VMEM((SHORT, 4 * BLOCK), F32),
            pltpu.VMEM((SHORT, 4 * BLOCK), BF),
        ],
        compiler_params=params(None),
        name="short",
    )(stok, projection, c_home, meta, table)

    grad, out, bias, stok_g, sgrad_g, short_out = pl.pallas_call(
        functools.partial(attend_kernel, n_dp),
        out_shape=(
            shaped((CHIPS, ROWS, BLOCK), BF),
            shaped((CHIPS, ROWS, HEAD), BF),
            shaped((LEVELS, 128), F32),
            shaped((CHIPS, SHORT, MODEL), BF),
            shaped((CHIPS, SHORT, BLOCK), BF),
            shaped((SHORT, BLOCK), BF),
        ),
        in_specs=[VM] * 11,
        out_specs=(VM,) * 6,
        scratch_shapes=[
            pltpu.VMEM((n_dp, SLEN, BLOCK), BF),
            pltpu.VMEM((CHIPS, 2 * CHIPS, ROWS, ROWS), BF),
            pltpu.VMEM((CHIPS, 2 * CHIPS, ROWS, ROWS), F32),
            pltpu.VMEM((CHIPS, ROWS, HEAD), F32),
            pltpu.VMEM((2 * CHIPS, ROWS, 128), BF),
            pltpu.VMEM((2 * CHIPS, ROWS, 128), F32),
            pltpu.VMEM((2 * CHIPS, 8, ROWS), F32),
            pltpu.VMEM((CHIPS, CHIPS, 8, ROWS), F32),
            pltpu.VMEM((2 * CHIPS, ROWS, HEAD), F32),
            pltpu.VMEM((2 * CHIPS, ROWS, HEAD), F32),
            pltpu.VMEM((ROWS, HEAD), F32),
            pltpu.VMEM((2, ROWS, 128), F32),
            pltpu.VMEM((8, ROWS), F32),
            pltpu.VMEM((CHIPS, ROWS, 2 * HEAD), BF),
            pltpu.VMEM((CHIPS, ROWS, 2 * HEAD), BF),
            DMA((CHIPS,)),
            DMA((CHIPS,)),
            DMA((CHIPS,)),
            DMA((CHIPS,)),
            DMA((n_dp,)),
            DMA((n_dp,)),
            DMA((CHIPS, CHIPS)),
            DMA((CHIPS, CHIPS)),
            DMA((CHIPS,)),
            DMA((CHIPS,)),
        ],
        compiler_params=params(1),
        name="attend",
    )(act, p_g, kv, c_g, times, table, stok, grad_heads, outbuf, place_m, sbias)

    part = MODEL // n_dp
    long_out, token_grad, proj_grad, bias_out = pl.pallas_call(
        functools.partial(finish_kernel, n_dp, part),
        out_shape=(
            shaped((ROWS, BLOCK), BF),
            shaped((ROWS, MODEL), BF),
            shaped((part, 2 * HEAD), F32),
            shaped((LEVELS, 128), F32),
        ),
        in_specs=[VM] * 6 + [ANY],
        out_specs=(VM,) * 4,
        scratch_shapes=[
            pltpu.VMEM((CHIPS, MODEL, BLOCK), BF),
            pltpu.VMEM((CHIPS, ROWS, BLOCK), BF),
            pltpu.VMEM((MODEL, 2 * HEAD), BF),
            pltpu.VMEM((MODEL, 2 * HEAD), BF),
            pltpu.VMEM((MODEL, 2 * HEAD), F32),
            pltpu.VMEM((n_dp, part, 2 * HEAD), BF),
            pltpu.VMEM((n_dp, part, 2 * HEAD), BF),
            pltpu.VMEM((n_dp, LEVELS, 128), F32),
            pltpu.VMEM((LEVELS, 128), F32),
            pltpu.VMEM((2 * CHIPS, LEVELS, 128), F32),
            pltpu.VMEM((part, 2 * HEAD), F32),
            DMA((4, 4)),
            DMA((CHIPS,)),
            DMA((CHIPS,)),
            DMA((CHIPS,)),
            DMA((CHIPS,)),
            DMA,
            DMA,
            DMA((n_dp,)),
            DMA((n_dp,)),
            DMA((n_dp,)),
            DMA((n_dp,)),
            DMA((2 * CHIPS,)),
            DMA((2 * CHIPS,)),
            DMA((2,)),
            DMA((2,)),
        ],
        compiler_params=params(2),
        name="finish",
    )(grad, out, tok_g, stok_g, sgrad_g, bias, projection)
    return (
        long_out[None],
        short_out.reshape(short_cotangent.shape),
        token_grad[None],
        short_grad.reshape(short_tokens.shape),
        proj_grad,
        jnp.transpose(bias_out[:, 0:4]),
    )


def solution(mesh):
    return jax.shard_map(
        functools.partial(per_device, mesh.shape["dp"]),
        mesh=mesh,
        in_specs=(
            P("dp", "ctx", None),
            P("dp", "ctx", None, None),
            P(),
            P(),
            P("dp"),
            P("dp", "ctx"),
            P("dp", "ctx"),
            P("dp", "ctx", None),
            P("dp", "ctx"),
            P("dp", "ctx", None),
            P("dp", "ctx", None, None),
        ),
        out_specs=(
            P("dp", "ctx", None),
            P("dp", "ctx", None, None),
            P("dp", "ctx", None),
            P("dp", "ctx", None, None),
            P("dp", "ctx"),
            P(),
        ),
        check_vma=False,
    )
```

time: 475 us -> 142 us (0.30)
  waiting for transfers between devices: 214 us -> 0 us
  Pallas kernels: 0 us -> 128 us
  blocking collectives: 92.6 us -> 0 us
  matrix products: 87.4 us -> 0 us
  starting transfers between devices: 25.5 us -> 0 us
  other arithmetic: 16.7 us -> 0 us
  between operations: 16.5 us -> 1.33 us
  local copies, waits for them, and re-layouts: 20 us -> 12.5 us
    reduce_scatter x4 -> x0, waiting for transfers between devices: 156 us -> none  [the longest x1 123 us: per_device(): lax.psum_scatter(lax.dot_general(all_tokens, all_grads, (((0,), (0,)), ((...]
    pallas_call x0 -> x4, Pallas kernels: none -> 128 us  [the longest x1 45.7 us: per_device(): pl.pallas_call(functools.partial(gather_kernel, n_dp), out_shape=(shaped(...]
    dot_general x26 -> x0, matrix products: 87.4 us -> none  [the longest x1 27.4 us: per_device(): jnp.einsum('rhd,chd->hrc', mixed_grad, value_rows, preferred_element_type...]
    psum x1 -> x0, blocking collectives: 80.8 us -> none  [per_device(): lax.psum(table_long + jnp.sum(short_table, axis=0), ('dp', 'ctx'))]
    all_to_all x4 -> x0, waiting for transfers between devices: 36.3 us -> none  [the longest x1 22.4 us: per_device(): lax.all_to_all(sent_tokens, 'dp', split_axis=0, concat_axis=0, tiled=True)]
    all_to_all x4 -> x0, starting transfers between devices: 24.8 us -> none  [the longest x1 9.57 us: per_device(): lax.all_to_all(routing, 'dp', split_axis=0, concat_axis=0, tiled=True)]
    all_gather x2 -> x0, waiting for transfers between devices: 22.4 us -> none  [the longest x1 13.8 us: per_device(): value_rows = lax.all_gather(values, 'ctx', axis=0, tiled=True)]
    all_gather x1 -> x0, blocking collectives: 11.9 us -> none  [per_device(): time_rows = lax.all_gather(own_time, 'ctx', axis=0, tiled=True)]
  transfers between devices with their start and end apart: 10 -> 0, of which waited for: 7 -> 0; matrix products, arithmetic and copies ran while one was open for 19% -> 0% of each run, Pallas kernels for 0% -> 0%
where the time goes in v1:
time: 142 us; the launch traced here: 141 us
  Pallas kernels  128 us (90%)
  local copies, waits for them, and re-layouts  12.5 us (9%)
    pallas_call x1, Pallas kernels, per_device(): pl.pallas_call(functools.partial(gather_kernel, n_dp), out_shape=(shaped(...  45.7 us
    pallas_call x1, Pallas kernels, per_device(): pl.pallas_call(functools.partial(attend_kernel, n_dp), out_shape=(shaped(...  41.5 us
    pallas_call x1, Pallas kernels, per_device(): pl.pallas_call(functools.partial(finish_kernel, n_dp, part), out_shape=(s...  33.5 us
    pallas_call x1, Pallas kernels, per_device(): pl.pallas_call(functools.partial(short_kernel, n_dp), out_shape=(shaped((...  6.96 us
    unnamed x7, local copies, waits for them, and re-layouts  6.22 us

profile of v1, /device:TPU:1, one launch (start us, length us, event | category | flops | bytes accessed | tf_op | source)
XLA Modules:
  0.0 141.4 jit_solution(4857950972543810870)
XLA Ops:
  1.3 0.8 reshape.34
  2.1 0.7 concatenate.6
  2.7 1.3 pad.5.table
  4.0 0.7 broadcast_in_dim.23
  4.7 0.1 broadcast_in_dim_reshape.6
  4.8 0.7 broadcast_in_dim.24
  5.5 0.1 broadcast_in_dim_reshape.7
  5.6 1.3 concatenate.7.meta
  6.9 45.7 %gather.1 = (bf16[4,256,1024]{2,1,0:T(8,128)(2,1)}, f32[4,256,512]{2,1,0:T(8,128)}, bf16[4,256,512]{2,1,0:T(8,128)(2,1)}, bf16[8,256,256]{2,1,0:T(8,128)(2,1)}, ...) custom-call(bf16[256,1024]{1,0:T(8,128)(2,1)} %bitcast.17, ...), custom_call_target="tpu_custom_call" | custom-call | tf_op jit(solution)/shard_map/gather/pallas_call | solution.py:959
  52.6 7.0 %short.1 = (bf16[128,1024]{1,0:T(8,128)(2,1)}, bf16[4,128,512]{2,1,0:T(8,128)(2,1)}, bf16[32,16,512]{2,1,0:T(8,128)(2,1)}, f32[16,128]{1,0:T(8,128)}) custom-call(bf16[128,1024]{1,0:T(8,128)(2,1)} %bitcast.15, bf16[1024,2048]{1,0:T(8,128)(2,1)} %w.5, bf16[128,512]{1,0:T(8,128)(2,1)} %get-tuple-element.33.cot, s32[8,128]{1,0:T(8,128)} %concatenate.7.meta, ...), custom_call_target="tpu_custom_call" | custom-call | tf_op jit(solution)/shard_map/short/pallas_call | solution.py:997
  59.5 41.5 %attend.1 = (bf16[4,256,512]{2,1,0:T(8,128)(2,1)}, bf16[4,256,128]{2,1,0:T(8,128)(2,1)}, f32[16,128]{1,0:T(8,128)}, bf16[4,128,1024]{2,1,0:T(8,128)(2,1)}, bf16[...) custom-call(bf16[4,256,512]{2,1,0:T(8,128)(2,1)} %get-tuple-element.28.act, f32[4,256,512]{2,1,0:T(8,128)} %get-tuple-element.29.p_g, ...), custom_call_target="tpu_custom_call" | custom-call | tf_op jit(solution)/shard_map/attend/pallas_call | solution.py:1015
  101.0 0.0 copy-start
  101.0 33.5 %finish.1 = (bf16[256,512]{1,0:T(8,128)(2,1)}, bf16[256,1024]{1,0:T(8,128)(2,1)}, f32[32,256]{1,0:T(8,128)}, f32[16,128]{1,0:T(8,128)}) custom-call(bf16[4,256,512]{2,1,0:T(8,128)(2,1)} %get-tuple-element.38.grad, bf16[4,256,128]{2,1,0:T(8,128)(2,1)} %get-tuple-element.39.out, bf16[4,256,1024]{2,1,0:T(8,128)(2,1)} %get-tuple-element.40.tok_g, ...), custom_call_target="tpu_custom_call" | custom-call | tf_op jit(solution)/shard_map/finish/pallas_call | solution.py:1059
  134.5 0.7 slice_bitcast_fusion
  135.2 0.7 copy.17
  135.8 1.7 %copy.23 = bf16[1,256,512]{2,1,0:T(8,128)(2,1)} copy(bf16[1,256,512]{2,1,0:T(8,128)(2,1)} %bitcast.20) | data formatting | bytes 524288
  137.5 0.0 copy-done
  137.5 0.7 copy.24
  138.2 1.9 %copy.25 = bf16[1,256,1024]{2,1,0:T(8,128)(2,1)} copy(bf16[1,256,1024]{2,1,0:T(8,128)(2,1)} %bitcast.18) | data formatting | bytes 1048576
  140.0 1.4 copy.26
  (2 shorter events, 0.0 us)
Async XLA Ops:
  101.0 36.5 %copy-start = (bf16[128,512]{1,0:T(8,128)(2,1)S(1)}, bf16[128,512]{1,0:T(8,128)(2,1)}, u32[]{:S(2)}) copy-start(bf16[128,512]{1,0:T(8,128)(2,1)} %get-tuple-element.45) | copy-start | bytes 393220

commit v2 on v0

v2 whole, which is shorter than its diff:
```python
import functools

import jax
import jax.numpy as jnp
from jax import lax
from jax.experimental import pallas as pl
from jax.experimental.pallas import tpu as pltpu
from jax.sharding import PartitionSpec as P

epsilon = 1e-05
MESH = pl.DeviceIdType.MESH
BF = jnp.bfloat16
F32 = jnp.float32
CHIPS = 4
ROWS = 256
HEAD = 128
LEVELS = 16
SLEN = 16
SHORT = 128
LONG_ROWS = CHIPS * ROWS
ALL_ROWS = CHIPS * (ROWS + SHORT)
PAIR = 2 * ROWS
MODEL = 1024
BLOCK = 512
SCALE = HEAD ** (-0.5)
VMEM_LIMIT = 56 * 1024 * 1024


def sigmoid(value):
    return 0.5 * jnp.tanh(0.5 * value) + 0.5


def silu_grad(value):
    sigma = sigmoid(value)
    return sigma * (1.0 + value * (1.0 - sigma))


def dot_nn(a, b):
    return jnp.dot(a, b, preferred_element_type=F32)


def dot_nt(a, b):
    return lax.dot_general(a, b, (((1,), (1,)), ((), ())), preferred_element_type=F32)


def dot_tn(a, b):
    return lax.dot_general(a, b, (((0,), (0,)), ((), ())), preferred_element_type=F32)


def column_of(row):
    return jnp.transpose(jnp.broadcast_to(row, (128, 128)))


def iota(shape, axis):
    return lax.broadcasted_iota(jnp.int32, shape, axis)


def remote(src, dst, send_sem, recv_sem, dp, ctx):
    return pltpu.make_async_remote_copy(
        src_ref=src,
        dst_ref=dst,
        send_sem=send_sem,
        recv_sem=recv_sem,
        device_id=(dp, ctx),
        device_id_type=MESH,
    )


def place():
    dp = lax.axis_index("dp")
    ctx = lax.axis_index("ctx")
    return dp, ctx, lax.div(ctx, 2), lax.rem(ctx, 2)


def lookup(table, diff):
    index = jnp.clip(diff, 0.0, LEVELS - 1.0).astype(jnp.int32)
    parts = [
        jnp.take_along_axis(table, index[:, i : i + 128], axis=1)
        for i in range(0, index.shape[1], 128)
    ]
    return parts[0] if len(parts) == 1 else jnp.concatenate(parts, axis=1)


def exact_dot(a, b):
    return lax.dot_general(
        a,
        b,
        (((1,), (0,)), ((), ())),
        precision=lax.Precision.HIGHEST,
        preferred_element_type=F32,
    )


def rows_at(block, rows):
    return pl.ds(pl.multiple_of(block * rows, rows), rows)


def lanes_at(block):
    return pl.ds(pl.multiple_of(block * HEAD, HEAD), HEAD)


def layer_kernel(
    n_dp,
    tok,
    stok,
    w,
    lcot,
    scot,
    ltime,
    stime,
    slen,
    dest_in,
    llen,
    tbias,
    long_out,
    short_out,
    token_grad,
    short_grad,
    proj_grad,
    bias_out,
    wh,
    tok_all,
    grad_all,
    p_s,
    act_s,
    kv,
    c_g,
    tmeta,
    times,
    tab_s,
    ints,
    dtile,
    dest_g,
    place_s,
    cbuf,
    crecv,
    sp_s,
    sact_s,
    sweight_s,
    sslope_s,
    snorm_s,
    sscale_s,
    c_home,
    sgrad_s,
    obuf,
    orecv,
    sbias_s,
    weight_s,
    slope_s,
    mixed_s,
    out_s,
    hot_s,
    tcol_s,
    stat_s,
    dk_s,
    dv_s,
    dq_s,
    hist_s,
    htot_s,
    tot_s,
    sib_send,
    sib_recv,
    grad_h,
    half_send,
    half_recv,
    own,
    rs_send,
    rs_recv,
    b_send,
    b_dp,
    b_mid,
    b_ctx,
    piece,
    w_sem,
    tok_s,
    tok_r,
    fwd_s,
    fwd_r,
    c_s,
    c_r,
    t_s,
    t_r,
    kv_s,
    kv_r,
    st_s,
    st_r,
    sg_s,
    sg_r,
    d_s,
    d_r,
    s_s,
    s_r,
    o_s,
    o_r,
    stat_ss,
    stat_sr,
    sib_s,
    sib_r,
    g_s,
    g_r,
    l_s,
    l_r,
    p_ss,
    p_sr,
    rs_s,
    rs_r,
    b1_s,
    b1_r,
    b2_s,
    b2_r,
    f_s,
    f_r,
):
    dp, ctx, chip, core = place()
    sib = ctx + 1 - 2 * core
    up = lax.rem(chip + 1, CHIPS)
    down = lax.rem(chip + CHIPS - 1, CHIPS)
    far = lax.rem(chip + 2, CHIPS)
    half_rows = ROWS // 2
    barrier = pltpu.get_barrier_semaphore()

    def greet_ctx(o, carry):
        pl.semaphore_signal(
            barrier, inc=1, device_id=(dp, lax.rem(ctx + o, 2 * CHIPS)), device_id_type=MESH
        )
        return carry

    def greet_dp(o, carry):
        pl.semaphore_signal(
            barrier, inc=1, device_id=(lax.rem(dp + o, n_dp), ctx), device_id_type=MESH
        )
        return carry

    lax.fori_loop(1, 2 * CHIPS, greet_ctx, 0)
    lax.fori_loop(1, n_dp, greet_dp, 0)

    def w_copy(h, k):
        return pltpu.make_async_copy(
            w.at[:, k * BLOCK + h * HEAD : k * BLOCK + (h + 1) * HEAD],
            wh.at[h, :, k * HEAD : (k + 1) * HEAD],
            w_sem.at[h, k],
        )

    for h in range(4):
        for k in range(4):
            w_copy(h, k).start()
    tmeta[...] = jnp.broadcast_to(ltime[...], (8, ROWS))
    ints[...] = jnp.zeros((8, 128), jnp.int32) - 1
    ints[0:1, 0:8] = slen[...]
    ints[1:2, 0:8] = dest_in[...]
    dtile[...] = jnp.broadcast_to(ints[1:2, :], (8, 128))
    tab_s[...] = jnp.zeros_like(tab_s)
    tab_s[0:4, 0:LEVELS] = tbias[...]

    def half_copy(peer, half, index):
        return remote(
            tok.at[half * half_rows : (half + 1) * half_rows, :],
            tok_all.at[rows_at(2 * chip + half, half_rows), :],
            tok_s.at[index, half],
            tok_r.at[index, half],
            dp,
            2 * peer + core,
        )

    def half_wait(src, half, index):
        here = tok_all.at[rows_at(2 * src + half, half_rows), :]
        remote(here, here, tok_s.at[index, half], tok_r.at[index, half], dp, sib).wait_recv()

    def pass_copy(src, half, peer):
        here = tok_all.at[rows_at(2 * src + half, half_rows), :]
        return remote(here, here, fwd_s.at[half], fwd_r.at[half], dp, 2 * peer + core)

    def c_copy(d):
        peer = lax.rem(chip + d, CHIPS)
        return remote(
            lcot.at[:, lanes_at(peer)], c_g.at[chip], c_s.at[d], c_r.at[d], dp, 2 * peer + core
        )

    def t_copy(o):
        return remote(
            tmeta, times.at[ctx], t_s.at[o], t_r.at[o], dp, lax.rem(ctx + o, 2 * CHIPS)
        )

    def kv_copy(src):
        here = kv.at[rows_at(2 * src + core, ROWS), :]
        return remote(here, here, kv_s.at[src], kv_r.at[src], dp, sib)

    def kv_wait(src):
        here = kv.at[rows_at(2 * src + 1 - core, ROWS), :]
        remote(here, here, kv_s.at[src], kv_r.at[src], dp, sib).wait_recv()

    def st_copy(d):
        return remote(
            stok,
            tok_all.at[pl.ds(pl.multiple_of(LONG_ROWS + chip * SHORT, SHORT), SHORT), :],
            st_s.at[d],
            st_r.at[d],
            dp,
            2 * lax.rem(chip + d, CHIPS) + core,
        )

    def sg_copy(d):
        peer = lax.rem(chip + d, CHIPS)
        return remote(
            sgrad_s.at[peer],
            grad_all.at[pl.ds(pl.multiple_of(LONG_ROWS + chip * SHORT, SHORT), SHORT), :],
            sg_s.at[d],
            sg_r.at[d],
            dp,
            2 * peer + core,
        )

    def dp_start(source, target, send, recv):
        def one(o, carry):
            peer = lax.rem(dp + o, n_dp)
            remote(source.at[peer], target.at[dp], send, recv, peer, ctx).start()
            return carry

        lax.fori_loop(1, n_dp, one, 0)

    def dp_all(source, target, send, recv):
        return remote(
            source.at[0 : n_dp - 1], target.at[0 : n_dp - 1], send, recv, dp, sib
        )

    def one_start(source, target, send, recv):
        def one(o, carry):
            remote(source, target.at[dp], send, recv, lax.rem(dp + o, n_dp), ctx).start()
            return carry

        lax.fori_loop(1, n_dp, one, 0)

    def one_all(target, send, recv):
        here = target.at[0 : n_dp - 1]
        return remote(here, here, send, recv, dp, sib)

    pl.semaphore_wait(barrier, n_dp - 1 + 2 * CHIPS - 1)
    half_copy(up, 0, 0).start()
    half_copy(down, 1, 1).start()
    half_copy(up, 1, 0).start()
    half_copy(down, 0, 1).start()
    one_start(dtile, dest_g, d_s, d_r)

    def start_t(o, carry):
        t_copy(o).start()
        return carry

    lax.fori_loop(1, 2 * CHIPS, start_t, 0)
    tok_all[rows_at(chip, ROWS), :] = tok[...]
    tok_all[pl.ds(pl.multiple_of(LONG_ROWS + chip * SHORT, SHORT), SHORT), :] = stok[...]
    c_g[chip] = lcot[:, lanes_at(chip)]
    times[ctx] = tmeta[...]
    dest_g[dp] = dtile[...]
    for h in range(4):
        for k in range(4):
            w_copy(h, k).wait()

    def project(src):
        projected = dot_nn(tok_all[rows_at(src, ROWS), :], wh[chip])
        p_s[src] = projected
        act = (projected * sigmoid(projected)).astype(BF)
        act_s[src] = act
        kv[rows_at(2 * src + core, ROWS), 0:HEAD] = act[:, 3 * HEAD : 4 * HEAD]
        kv[rows_at(2 * src + core, ROWS), HEAD : 2 * HEAD] = act[:, HEAD : 2 * HEAD]
        kv_copy(src).start()

    project(chip)

    lane16 = iota((16, 128), 1)
    spread_time = exact_dot(
        stime[0].astype(F32), jnp.where((lane16 & 15) == iota((16, 128), 0), 1.0, 0.0)
    )
    pick = (iota((8, 128), 1) >> 4) == iota((8, 128), 0)
    stime_row = jnp.sum(jnp.where(pick, spread_time, 0.0), axis=0, keepdims=True)
    repeat = jnp.where((iota((128, 128), 1) >> 4) == iota((128, 128), 0), 1.0, 0.0)
    rep_rows = exact_dot(ints[...].astype(F32), repeat)
    slen_row, home_row = rep_rows[0:1, :], rep_rows[1:2, :]
    owner_row = (home_row.astype(jnp.int32) >> 3).astype(F32)
    shape = (SHORT, SHORT)
    row = iota(shape, 0)
    col = iota(shape, 1)
    stime_diff = column_of(stime_row) - stime_row
    inside = (row & 15).astype(F32) < column_of(slen_row)
    svisible = ((row >> 4) == (col >> 4)) & (col <= row) & inside

    half_wait(down, 0, 0)
    pass_copy(down, 0, up).start()
    half_wait(up, 1, 1)
    pass_copy(up, 1, down).start()
    for d in (1, 3, 2):
        c_copy(d).start()

    one_all(dest_g, d_s, d_r).wait_recv()
    dest = dest_g[...]
    code = jnp.sum(
        jnp.where((dest >> 3) == dp, ((dest & 7) + 1).astype(F32), 0.0), axis=2, keepdims=True
    )
    code = jnp.broadcast_to(code, (n_dp, 8, 128))
    code = jnp.concatenate([code, code], axis=1).reshape(n_dp * SLEN, 128)
    shape = (n_dp * SLEN, 128)
    same = (iota(shape, 0) & 15) == (iota(shape, 1) & 15)
    slot = ((iota(shape, 1) >> 4) + 1).astype(F32)
    placer = jnp.where(same & (code == slot), 1.0, 0.0).astype(BF)
    place_s[...] = placer
    cbuf[...] = dot_nn(placer, scot[...]).astype(BF).reshape(cbuf.shape)
    dp_start(cbuf, crecv, s_s, s_r)
    crecv[dp] = cbuf[dp]

    short_tokens = stok[...]
    mixes = []
    for h in range(4):
        projected = dot_nn(short_tokens, wh[h])
        sp_s[h] = projected
        act = (projected * sigmoid(projected)).astype(BF)
        sact_s[h] = act
        queries, keys = act[:, 2 * HEAD : 3 * HEAD], act[:, 3 * HEAD : 4 * HEAD]
        tab = jnp.broadcast_to(tab_s[h : h + 1, :], (SHORT, 128))
        total = dot_nt(queries, keys) * SCALE + lookup(tab, stime_diff)
        sg = sigmoid(total)
        weight = total * sg
        weight16 = jnp.where(svisible, weight, 0.0).astype(BF)
        sweight_s[h] = weight16
        sslope_s[h] = jnp.where(svisible, sg + weight * (1.0 - sg), 0.0)
        mixes.append(dot_nn(weight16, act[:, HEAD : 2 * HEAD]))
    mean = sum(jnp.sum(m, axis=1, keepdims=True) for m in mixes) * (1.0 / BLOCK)
    centred = [m - mean for m in mixes]
    spread = sum(jnp.sum(m * m, axis=1, keepdims=True) for m in centred) * (1.0 / BLOCK)
    scale = lax.rsqrt(spread + epsilon)
    sscale_s[...] = jnp.broadcast_to(scale, sscale_s.shape)
    for h in range(4):
        snorm_s[h] = centred[h] * scale

    half_wait(down, 1, 0)
    project(down)
    half_wait(up, 0, 1)
    project(up)

    def wait_t(o, carry):
        src = lax.rem(ctx + 2 * CHIPS - o, 2 * CHIPS)
        remote(tmeta, times.at[src], t_s.at[o], t_r.at[o], dp, src).wait_recv()
        return carry

    lax.fori_loop(1, 2 * CHIPS, wait_t, 0)
    lane = iota((ROWS, 128), 1)

    def times_of(b, carry):
        line = times[b, 0:1, :].astype(F32)
        column = jnp.concatenate(
            [column_of(line[:, 0:128]), column_of(line[:, 128:256])], axis=0
        )
        tcol_s[b] = column
        hot_s[rows_at(b, ROWS), :] = jnp.where(
            (column.astype(jnp.int32) & 15) == lane, 1.0, 0.0
        ).astype(BF)
        return carry

    lax.fori_loop(0, 2 * CHIPS, times_of, 0)
    dk_s[...] = jnp.zeros_like(dk_s)
    dv_s[...] = jnp.zeros_like(dv_s)
    htot_s[...] = jnp.zeros_like(htot_s)
    tot_s[...] = jnp.zeros_like(tot_s)

    for half in range(2):
        here = tok_all.at[rows_at(2 * far + half, half_rows), :]
        remote(here, here, fwd_s.at[half], fwd_r.at[half], dp, sib).wait_recv()
    project(far)
    for d in (1, 3, 2):
        st_copy(d).start()
    for d in (1, 3, 2):
        src = lax.rem(chip + CHIPS - d, CHIPS)
        remote(c_g.at[src], c_g.at[src], c_s.at[d], c_r.at[d], dp, sib).wait_recv()
    for src in range(CHIPS):
        kv_wait(src)

    table = jnp.broadcast_to(tab_s[pl.ds(chip, 1), :], (ROWS, 128))
    length = llen[0]

    def stat_copy(qs, d):
        here = stat_s.at[qs, chip]
        return remote(
            here,
            here,
            stat_ss.at[qs, d],
            stat_sr.at[qs, d],
            dp,
            2 * lax.rem(chip + d, CHIPS) + core,
        )

    def key_times(p):
        return jnp.concatenate(
            [times[2 * p, 0:1, :], times[2 * p + 1, 0:1, :]], axis=1
        ).astype(F32)

    def forward(step, carry):
        qs = CHIPS - 1 - step
        block = 2 * qs + core
        queries = act_s[qs, :, 2 * HEAD : 3 * HEAD]
        tq = tcol_s[block][:, 0:1]
        spot = iota((ROWS, 1), 0) + block * ROWS
        limit = jnp.where(spot < length, spot, -1)
        mixed_s[qs] = jnp.zeros((ROWS, HEAD), F32)

        def tile(p, carry):
            keys = kv[rows_at(p, PAIR), 0:HEAD]
            values = kv[rows_at(p, PAIR), HEAD : 2 * HEAD]
            total = dot_nt(queries, keys) * SCALE + lookup(table, tq - key_times(p))
            sg = sigmoid(total)
            weight = total * sg
            visible = (iota((ROWS, PAIR), 1) + p * PAIR) <= limit
            weight16 = jnp.where(visible, weight, 0.0).astype(BF)
            weight_s[qs, p] = weight16
            slope_s[qs, p] = jnp.where(visible, sg + weight * (1.0 - sg), 0.0)
            mixed_s[qs] += dot_nn(weight16, values)
            return carry

        lax.fori_loop(0, qs + 1, tile, 0)
        mixed = mixed_s[qs]
        q = c_g[qs].astype(F32) * act_s[qs, :, 0:HEAD].astype(F32)
        s1 = jnp.sum(mixed, axis=1, keepdims=True)
        centred = mixed - s1 * (1.0 / HEAD)
        s2 = jnp.sum(centred * centred, axis=1, keepdims=True)
        s3 = jnp.sum(q, axis=1, keepdims=True)
        s4 = jnp.sum(q * centred, axis=1, keepdims=True)
        stats = jnp.where(
            lane == 0, s1, jnp.where(lane == 1, s2, jnp.where(lane == 2, s3, s4))
        )
        stat_s[qs, chip] = jnp.transpose(stats)[0:8, :]
        for d in (1, 3, 2):
            stat_copy(qs, d).start()
        return carry

    lax.fori_loop(0, CHIPS, forward, 0)

    dp_all(cbuf, crecv, s_s, s_r).wait_recv()
    owner = jnp.concatenate([column_of(owner_row)] * (n_dp * SLEN // 128), axis=1)
    shape = (SHORT, n_dp * SLEN)
    same = (iota(shape, 0) & 15) == (iota(shape, 1) & 15)
    chooser = jnp.where(
        same & (owner == (iota(shape, 1) >> 4).astype(F32)), 1.0, 0.0
    ).astype(BF)
    c_home[...] = dot_nn(chooser, crecv[...].reshape(n_dp * SLEN, BLOCK))
    scale = sscale_s[:, 0:1]
    mean_q = jnp.zeros((SHORT, 1), F32)
    mean_qn = jnp.zeros((SHORT, 1), F32)
    for h in range(4):
        q = c_home[:, h * HEAD : (h + 1) * HEAD] * sact_s[h, :, 0:HEAD].astype(F32)
        mean_q = mean_q + jnp.sum(q, axis=1, keepdims=True)
        mean_qn = mean_qn + jnp.sum(q * snorm_s[h], axis=1, keepdims=True)
    mean_q = mean_q * (1.0 / BLOCK)
    mean_qn = mean_qn * (1.0 / BLOCK)
    bucket = jnp.clip(stime_diff, 0.0, LEVELS - 1.0).astype(jnp.int32)
    level_lane = iota((LEVELS, 128), 1)
    sums = jnp.zeros((LEVELS, 128), F32)
    outs = []
    for h in range(4):
        act = sact_s[h]
        gates = act[:, 0:HEAD].astype(F32)
        values = act[:, HEAD : 2 * HEAD]
        queries = act[:, 2 * HEAD : 3 * HEAD]
        keys = act[:, 3 * HEAD : 4 * HEAD]
        normed = snorm_s[h]
        cot = c_home[:, h * HEAD : (h + 1) * HEAD]
        outs.append((normed * gates).astype(BF))
        mixed_grad = ((cot * gates - mean_q - normed * mean_qn) * scale).astype(BF)
        score = dot_nt(mixed_grad, values) * sslope_s[h]
        rows = [
            jnp.sum(jnp.where(bucket == b, score, 0.0), axis=0, keepdims=True)
            for b in range(LEVELS)
        ]
        per_level = jnp.sum(jnp.concatenate(rows, axis=0), axis=1, keepdims=True)
        sums = sums + jnp.where(level_lane == h, per_level, 0.0)
        half = score.astype(BF)
        grads = [
            cot * normed,
            dot_tn(sweight_s[h], mixed_grad),
            dot_nn(half, keys) * SCALE,
            dot_tn(half, queries) * SCALE,
        ]
        for k in range(4):
            lanes = slice(k * HEAD, (k + 1) * HEAD)
            sgrad_s[h, :, lanes] = (grads[k] * silu_grad(sp_s[h, :, lanes])).astype(BF)
    sbias_s[...] = sums
    shape = (n_dp * SLEN, SHORT)
    same = (iota(shape, 0) & 15) == (iota(shape, 1) & 15)
    sender = jnp.where(
        same & (owner_row == (iota(shape, 0) >> 4).astype(F32)), 1.0, 0.0
    ).astype(BF)
    obuf[...] = dot_nn(sender, jnp.concatenate(outs, axis=1)).astype(BF).reshape(obuf.shape)
    for d in (1, 3, 2):
        sg_copy(d).start()
    grad_all[pl.ds(pl.multiple_of(LONG_ROWS + chip * SHORT, SHORT), SHORT), :] = sgrad_s[chip]
    dp_start(obuf, orecv, o_s, o_r)
    orecv[dp] = obuf[dp]

    def sib_copy(qs):
        return remote(
            sib_send.at[qs], sib_recv.at[qs], sib_s.at[qs], sib_r.at[qs], dp, sib
        )

    def g_copy(k, qs):
        return remote(
            grad_all.at[rows_at(qs, ROWS), k * HEAD : (k + 1) * HEAD],
            grad_h.at[chip, :, k * HEAD : (k + 1) * HEAD],
            g_s.at[k, qs],
            g_r.at[k, chip],
            dp,
            2 * qs + core,
        )

    def l_copy(qs):
        return remote(
            out_s.at[qs], long_out.at[:, lanes_at(chip)], l_s.at[qs], l_r.at[chip], dp, 2 * qs + core
        )

    def backward(step, carry):
        qs = CHIPS - 1 - step
        block = 2 * qs + core
        mine = rows_at(qs, ROWS)
        for d in (1, 3, 2):
            here = stat_s.at[qs, lax.rem(chip + CHIPS - d, CHIPS)]
            remote(here, here, stat_ss.at[qs, d], stat_sr.at[qs, d], dp, sib).wait_recv()
        stats = [stat_s[qs, h] for h in range(4)]
        mean = sum(s[0:1, :] for s in stats) * (1.0 / BLOCK)
        gaps = [s[0:1, :] * (1.0 / HEAD) - mean for s in stats]
        spread = sum(s[1:2, :] + HEAD * g * g for s, g in zip(stats, gaps)) * (1.0 / BLOCK)
        scale = lax.rsqrt(spread + epsilon)
        mean_q = sum(s[2:3, :] for s in stats) * (1.0 / BLOCK)
        mean_qn = sum(s[3:4, :] + g * s[2:3, :] for s, g in zip(stats, gaps))
        mean_qn = mean_qn * scale * (1.0 / BLOCK)
        whole = jnp.concatenate(
            [mean, scale, mean_q, mean_qn, jnp.zeros((124, ROWS), F32)], axis=0
        )
        cols = jnp.transpose(whole)
        mean, scale = cols[:, 0:1], cols[:, 1:2]
        mean_q, mean_qn = cols[:, 2:3], cols[:, 3:4]
        normed = (mixed_s[qs] - mean) * scale
        gates = act_s[qs, :, 0:HEAD].astype(F32)
        cotangent = c_g[qs].astype(F32)
        out_s[qs] = (normed * gates).astype(BF)
        mixed_grad = ((cotangent * gates - mean_q - normed * mean_qn) * scale).astype(BF)
        grad_all[mine, 0:HEAD] = (cotangent * normed * silu_grad(p_s[qs, :, 0:HEAD])).astype(BF)

        @pl.when(qs != chip)
        def _():
            l_copy(qs).start()
            g_copy(0, qs).start()

        queries = act_s[qs, :, 2 * HEAD : 3 * HEAD]
        tq = tcol_s[block][:, 0:1]
        dq_s[...] = jnp.zeros_like(dq_s)
        hist_s[...] = jnp.zeros_like(hist_s)

        def tile(p, carry):
            span = rows_at(p, PAIR)
            keys = kv[span, 0:HEAD]
            values = kv[span, HEAD : 2 * HEAD]
            score = dot_nt(mixed_grad, values) * slope_s[qs, p]
            near = jnp.where(tq - key_times(p) < LEVELS - 1.0, score, 0.0).astype(BF)
            half = score.astype(BF)
            tot_s[...] += jnp.sum(score.reshape(ROWS // 8, 8, PAIR), axis=0)
            hist_s[...] += dot_nn(near, hot_s[span, :])
            dq_s[...] += dot_nn(half, keys)
            dk_s[span, :] += dot_tn(half, queries)
            dv_s[span, :] += dot_tn(weight_s[qs, p], mixed_grad)
            return carry

        lax.fori_loop(0, qs + 1, tile, 0)
        htot_s[...] += lax.dot_general(
            hot_s[rows_at(block, ROWS), :].astype(F32),
            hist_s[...],
            (((0,), (0,)), ((), ())),
            precision=lax.Precision.HIGHEST,
            preferred_element_type=F32,
        )
        grad_all[mine, 2 * HEAD : 3 * HEAD] = (
            dq_s[...] * SCALE * silu_grad(p_s[qs, :, 2 * HEAD : 3 * HEAD])
        ).astype(BF)
        other = rows_at(2 * qs + 1 - core, ROWS)
        sib_send[qs, :, 0:HEAD] = dk_s[other, :].astype(BF)
        sib_send[qs, :, HEAD : 2 * HEAD] = dv_s[other, :].astype(BF)
        sib_copy(qs).start()

        @pl.when(qs != chip)
        def _():
            g_copy(2, qs).start()

        return carry

    lax.fori_loop(0, CHIPS, backward, 0)

    def finish(step, carry):
        qs = CHIPS - 1 - step
        sib_copy(qs).wait_recv()
        mine = rows_at(qs, ROWS)
        block = rows_at(2 * qs + core, ROWS)
        dk = (dk_s[block, :] + sib_recv[qs, :, 0:HEAD].astype(F32)) * SCALE
        dv = dv_s[block, :] + sib_recv[qs, :, HEAD : 2 * HEAD].astype(F32)
        grad_all[mine, HEAD : 2 * HEAD] = (
            dv * silu_grad(p_s[qs, :, HEAD : 2 * HEAD])
        ).astype(BF)
        grad_all[mine, 3 * HEAD : 4 * HEAD] = (
            dk * silu_grad(p_s[qs, :, 3 * HEAD : 4 * HEAD])
        ).astype(BF)

        @pl.when(qs != chip)
        def _():
            g_copy(1, qs).start()
            g_copy(3, qs).start()

        return carry

    lax.fori_loop(0, CHIPS, finish, 0)

    for d in (1, 3, 2):
        src = lax.rem(chip + CHIPS - d, CHIPS)
        there = pl.ds(pl.multiple_of(LONG_ROWS + src * SHORT, SHORT), SHORT)
        remote(stok, tok_all.at[there, :], st_s.at[d], st_r.at[d], dp, sib).wait_recv()
        remote(sgrad_s.at[src], grad_all.at[there, :], sg_s.at[d], sg_r.at[d], dp, sib).wait_recv()

    def outer(pair):
        cols = pl.ds(pl.multiple_of(pair * 2 * HEAD, 2 * HEAD), 2 * HEAD)
        return dot_tn(tok_all[...], grad_all[:, cols])

    half_send[...] = outer(1 - core).astype(BF)
    swap = remote(half_send, half_recv, p_ss, p_sr, dp, sib)
    swap.start()
    own[...] = outer(core)
    swap.wait_recv()
    rs_send[...] = (own[...] + half_recv[...].astype(F32)).astype(BF).reshape(rs_send.shape)
    dp_start(rs_send, rs_recv, rs_s, rs_r)
    rs_recv[dp] = rs_send[dp]

    shape = (128, 128)
    gap = (iota(shape, 0) - iota(shape, 1)) & 15
    hist = htot_s[...]
    rows = [
        jnp.sum(jnp.where(gap == b, hist, 0.0), axis=0, keepdims=True) for b in range(LEVELS - 1)
    ]
    total = jnp.sum(tot_s[...], axis=0, keepdims=True)
    total = sum(total[:, i : i + 128] for i in range(0, PAIR, 128))
    rows.append(total - sum(rows))
    levels = jnp.sum(jnp.concatenate(rows, axis=0), axis=1, keepdims=True)
    levels = sbias_s[...] + jnp.where(level_lane == chip, levels, 0.0)
    levels = jnp.concatenate([levels, jnp.zeros((128 - LEVELS, 128), F32)], axis=0)
    b_send[...] = jnp.transpose(levels)[0:8, :]
    one_start(b_send, b_dp, b1_s, b1_r)
    b_dp[dp] = b_send[...]

    dp_all(obuf, orecv, o_s, o_r).wait_recv()
    short_out[...] = dot_tn(place_s[...], orecv[...].reshape(n_dp * SLEN, BLOCK)).astype(BF)
    total = dot_nt(sgrad_s[0], wh[0])
    for h in range(1, 4):
        total = total + dot_nt(sgrad_s[h], wh[h])
    short_grad[...] = total.astype(BF)

    one_all(b_dp, b1_s, b1_r).wait_recv()
    b_mid[...] = jnp.sum(b_dp[...], axis=0)

    def b2_copy(o):
        return remote(
            b_mid, b_ctx.at[ctx], b2_s.at[o], b2_r.at[o], dp, lax.rem(ctx + o, 2 * CHIPS)
        )

    def start_b2(o, carry):
        b2_copy(o).start()
        return carry

    lax.fori_loop(1, 2 * CHIPS, start_b2, 0)
    b_ctx[ctx] = b_mid[...]

    long_out[:, lanes_at(chip)] = out_s[chip]
    grad_h[chip] = grad_all[rows_at(chip, ROWS), :]
    total = dot_nt(grad_h[chip], wh[chip])
    for d in (1, 3, 2):
        src = lax.rem(chip + CHIPS - d, CHIPS)
        for k in range(4):
            here = grad_h.at[src, :, k * HEAD : (k + 1) * HEAD]
            remote(here, here, g_s.at[k, src], g_r.at[k, src], dp, sib).wait_recv()
        here = long_out.at[:, lanes_at(src)]
        remote(out_s.at[src], here, l_s.at[src], l_r.at[src], dp, sib).wait_recv()
        total = total + dot_nt(grad_h[src], wh[src])
    token_grad[...] = total.astype(BF)

    def wait_b2(o, carry):
        src = lax.rem(ctx + 2 * CHIPS - o, 2 * CHIPS)
        remote(b_mid, b_ctx.at[src], b2_s.at[o], b2_r.at[o], dp, src).wait_recv()
        return carry

    lax.fori_loop(1, 2 * CHIPS, wait_b2, 0)
    bias_out[...] = jnp.sum(b_ctx[...], axis=0)[0:4, 0:LEVELS]

    half_copy(up, 0, 0).wait_send()
    half_copy(up, 1, 0).wait_send()
    half_copy(down, 0, 1).wait_send()
    half_copy(down, 1, 1).wait_send()
    pass_copy(down, 0, up).wait_send()
    pass_copy(up, 1, down).wait_send()
    for d in (1, 3, 2):
        c_copy(d).wait_send()
        st_copy(d).wait_send()
        sg_copy(d).wait_send()
    one_all(dest_g, d_s, d_r).wait_send()
    dp_all(cbuf, crecv, s_s, s_r).wait_send()
    dp_all(obuf, orecv, o_s, o_r).wait_send()
    one_all(b_dp, b1_s, b1_r).wait_send()

    def ended_o(o, carry):
        t_copy(o).wait_send()
        b2_copy(o).wait_send()
        return carry

    lax.fori_loop(1, 2 * CHIPS, ended_o, 0)

    def ended_q(qs, carry):
        kv_copy(qs).wait_send()
        sib_copy(qs).wait_send()
        for d in (1, 3, 2):
            stat_copy(qs, d).wait_send()

        @pl.when(qs != chip)
        def _():
            l_copy(qs).wait_send()
            for k in range(4):
                g_copy(k, qs).wait_send()

        return carry

    lax.fori_loop(0, CHIPS, ended_q, 0)
    swap.wait_send()

    dp_all(rs_send, rs_recv, rs_s, rs_r).wait_recv()
    piece[...] = jnp.sum(rs_recv[...].astype(F32), axis=0)
    mine = lax.rem(chip, 2)

    def f_copy(i):
        target = 2 * (2 * core + i) + lax.div(chip, 2)
        return target, remote(
            piece.at[:, i * HEAD : (i + 1) * HEAD],
            proj_grad.at[:, lanes_at(mine)],
            f_s.at[i],
            f_r.at[mine],
            dp,
            target,
        )

    for i in range(2):
        target, copy = f_copy(i)

        @pl.when(target != ctx)
        def _():
            copy.start()

        @pl.when(target == ctx)
        def _():
            proj_grad[:, lanes_at(mine)] = piece[:, i * HEAD : (i + 1) * HEAD]

    for half in range(2):
        source = 2 * (2 * core + half) + lax.div(chip, 2)

        @pl.when(source != ctx)
        def _():
            remote(
                piece.at[:, 0:HEAD],
                proj_grad.at[:, half * HEAD : (half + 1) * HEAD],
                f_s.at[half],
                f_r.at[half],
                dp,
                source,
            ).wait_recv()

    for i in range(2):
        target, copy = f_copy(i)

        @pl.when(target != ctx)
        def _():
            copy.wait_send()

    dp_all(rs_send, rs_recv, rs_s, rs_r).wait_send()


def output_kernel(count, *refs):
    for i in range(count):
        refs[count + i][...] = refs[i][...]


VM = pl.BlockSpec(memory_space=pltpu.VMEM)
SM = pl.BlockSpec(memory_space=pltpu.SMEM)
ANY = pl.BlockSpec(memory_space=pl.ANY)
DMA = pltpu.SemaphoreType.DMA
VMEM = pltpu.VMEM


def shaped(shape, dtype):
    return jax.ShapeDtypeStruct(shape, dtype)


def per_device(
    n_dp,
    long_tokens,
    short_tokens,
    projection,
    time_bias,
    long_length,
    short_length,
    long_time,
    short_time,
    destination,
    long_cotangent,
    short_cotangent,
):
    part = MODEL // n_dp
    spread = (n_dp, SLEN, BLOCK)
    scratch = [
        VMEM((CHIPS, MODEL, BLOCK), BF),
        VMEM((ALL_ROWS, MODEL), BF),
        VMEM((ALL_ROWS, BLOCK), BF),
        VMEM((CHIPS, ROWS, BLOCK), F32),
        VMEM((CHIPS, ROWS, BLOCK), BF),
        VMEM((2 * CHIPS * ROWS, 2 * HEAD), BF),
        VMEM((CHIPS, ROWS, HEAD), BF),
        VMEM((8, ROWS), jnp.int32),
        VMEM((2 * CHIPS, 8, ROWS), jnp.int32),
        VMEM((8, 128), F32),
        VMEM((8, 128), jnp.int32),
        VMEM((8, 128), jnp.int32),
        VMEM((n_dp, 8, 128), jnp.int32),
        VMEM((n_dp * SLEN, 128), BF),
        VMEM(spread, BF),
        VMEM(spread, BF),
        VMEM((4, SHORT, BLOCK), F32),
        VMEM((4, SHORT, BLOCK), BF),
        VMEM((4, SHORT, SHORT), BF),
        VMEM((4, SHORT, SHORT), F32),
        VMEM((4, SHORT, HEAD), F32),
        VMEM((SHORT, 128), F32),
        VMEM((SHORT, BLOCK), F32),
        VMEM((4, SHORT, BLOCK), BF),
        VMEM(spread, BF),
        VMEM(spread, BF),
        VMEM((LEVELS, 128), F32),
        VMEM((CHIPS, CHIPS, ROWS, PAIR), BF),
        VMEM((CHIPS, CHIPS, ROWS, PAIR), F32),
        VMEM((CHIPS, ROWS, HEAD), F32),
        VMEM((CHIPS, ROWS, HEAD), BF),
        VMEM((2 * CHIPS * ROWS, 128), BF),
        VMEM((2 * CHIPS, ROWS, 128), F32),
        VMEM((CHIPS, CHIPS, 8, ROWS), F32),
        VMEM((2 * CHIPS * ROWS, HEAD), F32),
        VMEM((2 * CHIPS * ROWS, HEAD), F32),
        VMEM((ROWS, HEAD), F32),
        VMEM((ROWS, 128), F32),
        VMEM((128, 128), F32),
        VMEM((8, PAIR), F32),
        VMEM((CHIPS, ROWS, 2 * HEAD), BF),
        VMEM((CHIPS, ROWS, 2 * HEAD), BF),
        VMEM((CHIPS, ROWS, BLOCK), BF),
        VMEM((MODEL, 2 * HEAD), BF),
        VMEM((MODEL, 2 * HEAD), BF),
        VMEM((MODEL, 2 * HEAD), F32),
        VMEM((n_dp, part, 2 * HEAD), BF),
        VMEM((n_dp, part, 2 * HEAD), BF),
        VMEM((8, 128), F32),
        VMEM((n_dp, 8, 128), F32),
        VMEM((8, 128), F32),
        VMEM((2 * CHIPS, 8, 128), F32),
        VMEM((part, 2 * HEAD), F32),
        DMA((4, 4)),
        DMA((2, 2)),
        DMA((2, 2)),
        DMA((2,)),
        DMA((2,)),
        DMA((CHIPS,)),
        DMA((CHIPS,)),
        DMA((2 * CHIPS,)),
        DMA((2 * CHIPS,)),
        DMA((CHIPS,)),
        DMA((CHIPS,)),
        DMA((CHIPS,)),
        DMA((CHIPS,)),
        DMA((CHIPS,)),
        DMA((CHIPS,)),
        DMA,
        DMA,
        DMA,
        DMA,
        DMA,
        DMA,
        DMA((CHIPS, CHIPS)),
        DMA((CHIPS, CHIPS)),
        DMA((CHIPS,)),
        DMA((CHIPS,)),
        DMA((4, CHIPS)),
        DMA((4, CHIPS)),
        DMA((CHIPS,)),
        DMA((CHIPS,)),
        DMA,
        DMA,
        DMA,
        DMA,
        DMA,
        DMA,
        DMA((2 * CHIPS,)),
        DMA((2 * CHIPS,)),
        DMA((2,)),
        DMA((2,)),
    ]
    results = pl.pallas_call(
        functools.partial(layer_kernel, n_dp),
        out_shape=(
            shaped((ROWS, BLOCK), BF),
            shaped((SHORT, BLOCK), BF),
            shaped((ROWS, MODEL), BF),
            shaped((SHORT, MODEL), BF),
            shaped((part, 2 * HEAD), F32),
            shaped(time_bias.shape, F32),
        ),
        in_specs=[VM, VM, ANY, VM, VM, VM, VM, VM, VM, SM, VM],
        out_specs=(VM,) * 6,
        scratch_shapes=scratch,
        compiler_params=pltpu.CompilerParams(
            vmem_limit_bytes=VMEM_LIMIT, collective_id=0, has_side_effects=True
        ),
        name="layer",
    )(
        long_tokens[0],
        short_tokens.reshape(SHORT, MODEL),
        projection,
        long_cotangent[0],
        short_cotangent.reshape(SHORT, BLOCK),
        long_time,
        short_time,
        short_length,
        destination,
        long_length,
        time_bias,
    )
    results = pl.pallas_call(
        functools.partial(output_kernel, len(results)),
        out_shape=tuple(shaped(r.shape, r.dtype) for r in results),
        in_specs=[VM] * len(results),
        out_specs=(VM,) * len(results),
        compiler_params=pltpu.CompilerParams(vmem_limit_bytes=VMEM_LIMIT),
        name="output",
    )(*results)
    long_out, short_out, token_grad, short_grad, proj_grad, bias_out = results
    return (
        long_out[None],
        short_out.reshape(short_cotangent.shape),
        token_grad[None],
        short_grad.reshape(short_tokens.shape),
        proj_grad,
        bias_out,
    )


def solution(mesh):
    return jax.shard_map(
        functools.partial(per_device, mesh.shape["dp"]),
        mesh=mesh,
        in_specs=(
            P("dp", "ctx", None),
            P("dp", "ctx", None, None),
            P(),
            P(),
            P("dp"),
            P("dp", "ctx"),
            P("dp", "ctx"),
            P("dp", "ctx", None),
            P("dp", "ctx"),
            P("dp", "ctx", None),
            P("dp", "ctx", None, None),
        ),
        out_specs=(
            P("dp", "ctx", None),
            P("dp", "ctx", None, None),
            P("dp", "ctx", None),
            P("dp", "ctx", None, None),
            P("dp", "ctx"),
            P(),
        ),
        check_vma=False,
    )
```

time: 475 us -> 93.4 us (0.20)
  waiting for transfers between devices: 214 us -> 0 us
  blocking collectives: 92.6 us -> 0 us
  Pallas kernels: 0 us -> 92 us
  matrix products: 87.4 us -> 0 us
  starting transfers between devices: 25.5 us -> 0 us
  local copies, waits for them, and re-layouts: 20 us -> 0 us
  other arithmetic: 16.7 us -> 0 us
  between operations: 16.5 us -> 1.29 us
    reduce_scatter x4 -> x0, waiting for transfers between devices: 156 us -> none  [the longest x1 123 us: per_device(): lax.psum_scatter(lax.dot_general(all_tokens, all_grads, (((0,), (0,)), ((...]
    pallas_call x0 -> x2, Pallas kernels: none -> 92 us  [the longest x1 89.7 us: per_device(): pl.pallas_call(functools.partial(layer_kernel, n_dp), out_shape=(shaped((...]
    dot_general x26 -> x0, matrix products: 87.4 us -> none  [the longest x1 27.4 us: per_device(): jnp.einsum('rhd,chd->hrc', mixed_grad, value_rows, preferred_element_type...]
    psum x1 -> x0, blocking collectives: 80.8 us -> none  [per_device(): lax.psum(table_long + jnp.sum(short_table, axis=0), ('dp', 'ctx'))]
    all_to_all x4 -> x0, waiting for transfers between devices: 36.3 us -> none  [the longest x1 22.4 us: per_device(): lax.all_to_all(sent_tokens, 'dp', split_axis=0, concat_axis=0, tiled=True)]
    all_to_all x4 -> x0, starting transfers between devices: 24.8 us -> none  [the longest x1 9.57 us: per_device(): lax.all_to_all(routing, 'dp', split_axis=0, concat_axis=0, tiled=True)]
    all_gather x2 -> x0, waiting for transfers between devices: 22.4 us -> none  [the longest x1 13.8 us: per_device(): value_rows = lax.all_gather(values, 'ctx', axis=0, tiled=True)]
    unnamed x224 -> x0, local copies, waits for them, and re-layouts: 12.5 us -> none
  transfers between devices with their start and end apart: 10 -> 0, of which waited for: 7 -> 0; matrix products, arithmetic and copies ran while one was open for 19% -> 0% of each run, Pallas kernels for 0% -> 0%
where the time goes in v2:
time: 93.4 us; the launch traced here: 93.3 us
  Pallas kernels  92 us (99%)
  between operations  1.29 us (1%)
    pallas_call x1, Pallas kernels, per_device(): pl.pallas_call(functools.partial(layer_kernel, n_dp), out_shape=(shaped((...  89.7 us
    pallas_call x1, Pallas kernels, per_device(): pl.pallas_call(functools.partial(output_kernel, len(results)), out_shape=...  2.3 us

profile of v2, /device:TPU:1, one launch (start us, length us, event | category | flops | bytes accessed | tf_op | source)
XLA Modules:
  0.0 93.3 jit_solution(7933012893867269629)
XLA Ops:
  1.3 89.7 %layer.1 = (bf16[256,512]{1,0:T(8,128)(2,1)}, bf16[128,512]{1,0:T(8,128)(2,1)}, bf16[256,1024]{1,0:T(8,128)(2,1)}, bf16[128,1024]{1,0:T(8,128)(2,1)}, f32[32,256]{1,0:T(8,128)}, /*index=5*/f32[4,16]{1,0:T(4,128)}) custom-call(bf16[256,1024]{1,0:T(8,128)(2,1)} %bitcast.8, bf16[128,1024]{1,0:T(8,128)(2,1)} %bitcast.9, bf16[1024,2048]{1,0:T(8,128)(2,1)} %w.1, ...), custom_call_target="tpu_custom_call" | custom-call | tf_op jit(solution)/shard_map/layer/pallas_call | solution.py:1007
  91.0 2.3 %output.1 = (bf16[256,512]{1,0:T(8,128)(2,1)}, bf16[128,512]{1,0:T(8,128)(2,1)}, bf16[256,1024]{1,0:T(8,128)(2,1)}, bf16[128,1024]{1,0:T(8,128)(2,1)}, f32[32,256]{1,0:T(8,128)}, /*index=5*/f32[4,16]{1,0:T(4,128)}) custom-call(bf16[256,512]{1,0:T(8,128)(2,1)} %get-tuple-element.18.refs_0_, bf16[128,512]{1,0:T(8,128)(2,1)} %get-tuple-element.19.refs_1_, ...), custom_call_target="tpu_custom_call" | custom-call | tf_op jit(solution)/shard_map/output/pallas_call | solution.py:1037

commit v3 on v2

--- a/solution.py
+++ b/solution.py
@@ -30,9 +30,10 @@
     return 0.5 * jnp.tanh(0.5 * value) + 0.5
 
 
-def silu_grad(value):
+def silu_and_grad(value):
     sigma = sigmoid(value)
-    return sigma * (1.0 + value * (1.0 - sigma))
+    silu = value * sigma
+    return silu.astype(BF), sigma + silu * (1.0 - sigma)
 
 
 def dot_nn(a, b):
@@ -171,7 +172,13 @@
     b_mid,
     b_ctx,
     piece,
+    lo_v,
+    so_v,
+    tg_v,
+    sg_v,
     w_sem,
+    in_sem,
+    out_sem,
     tok_s,
     tok_r,
     fwd_s,
@@ -334,6 +341,14 @@
         here = target.at[0 : n_dp - 1]
         return remote(here, here, send, recv, dp, sib)
 
+    home_rows = pl.ds(pl.multiple_of(LONG_ROWS + chip * SHORT, SHORT), SHORT)
+    loads = [
+        pltpu.make_async_copy(tok, tok_all.at[rows_at(chip, ROWS), :], in_sem.at[0]),
+        pltpu.make_async_copy(stok, tok_all.at[home_rows, :], in_sem.at[1]),
+        pltpu.make_async_copy(lcot.at[:, lanes_at(chip)], c_g.at[chip], in_sem.at[2]),
+    ]
+    for load in loads:
+        load.start()
     pl.semaphore_wait(barrier, n_dp - 1 + 2 * CHIPS - 1)
     half_copy(up, 0, 0).start()
     half_copy(down, 1, 1).start()
@@ -346,19 +361,17 @@
         return carry
 
     lax.fori_loop(1, 2 * CHIPS, start_t, 0)
-    tok_all[rows_at(chip, ROWS), :] = tok[...]
-    tok_all[pl.ds(pl.multiple_of(LONG_ROWS + chip * SHORT, SHORT), SHORT), :] = stok[...]
-    c_g[chip] = lcot[:, lanes_at(chip)]
     times[ctx] = tmeta[...]
     dest_g[dp] = dtile[...]
     for h in range(4):
         for k in range(4):
             w_copy(h, k).wait()
+    for load in loads:
+        load.wait()
 
     def project(src):
         projected = dot_nn(tok_all[rows_at(src, ROWS), :], wh[chip])
-        p_s[src] = projected
-        act = (projected * sigmoid(projected)).astype(BF)
+        act, p_s[src] = silu_and_grad(projected)
         act_s[src] = act
         kv[rows_at(2 * src + core, ROWS), 0:HEAD] = act[:, 3 * HEAD : 4 * HEAD]
         kv[rows_at(2 * src + core, ROWS), HEAD : 2 * HEAD] = act[:, HEAD : 2 * HEAD]
@@ -383,35 +396,10 @@
     inside = (row & 15).astype(F32) < column_of(slen_row)
     svisible = ((row >> 4) == (col >> 4)) & (col <= row) & inside
 
-    half_wait(down, 0, 0)
-    pass_copy(down, 0, up).start()
-    half_wait(up, 1, 1)
-    pass_copy(up, 1, down).start()
-    for d in (1, 3, 2):
-        c_copy(d).start()
-
-    one_all(dest_g, d_s, d_r).wait_recv()
-    dest = dest_g[...]
-    code = jnp.sum(
-        jnp.where((dest >> 3) == dp, ((dest & 7) + 1).astype(F32), 0.0), axis=2, keepdims=True
-    )
-    code = jnp.broadcast_to(code, (n_dp, 8, 128))
-    code = jnp.concatenate([code, code], axis=1).reshape(n_dp * SLEN, 128)
-    shape = (n_dp * SLEN, 128)
-    same = (iota(shape, 0) & 15) == (iota(shape, 1) & 15)
-    slot = ((iota(shape, 1) >> 4) + 1).astype(F32)
-    placer = jnp.where(same & (code == slot), 1.0, 0.0).astype(BF)
-    place_s[...] = placer
-    cbuf[...] = dot_nn(placer, scot[...]).astype(BF).reshape(cbuf.shape)
-    dp_start(cbuf, crecv, s_s, s_r)
-    crecv[dp] = cbuf[dp]
-
-    short_tokens = stok[...]
+    short_tokens = tok_all[home_rows, :]
     mixes = []
     for h in range(4):
-        projected = dot_nn(short_tokens, wh[h])
-        sp_s[h] = projected
-        act = (projected * sigmoid(projected)).astype(BF)
+        act, sp_s[h] = silu_and_grad(dot_nn(short_tokens, wh[h]))
         sact_s[h] = act
         queries, keys = act[:, 2 * HEAD : 3 * HEAD], act[:, 3 * HEAD : 4 * HEAD]
         tab = jnp.broadcast_to(tab_s[h : h + 1, :], (SHORT, 128))
@@ -430,10 +418,28 @@
     for h in range(4):
         snorm_s[h] = centred[h] * scale
 
-    half_wait(down, 1, 0)
-    project(down)
-    half_wait(up, 0, 1)
-    project(up)
+    one_all(dest_g, d_s, d_r).wait_recv()
+    dest = dest_g[...]
+    code = jnp.sum(
+        jnp.where((dest >> 3) == dp, ((dest & 7) + 1).astype(F32), 0.0), axis=2, keepdims=True
+    )
+    code = jnp.broadcast_to(code, (n_dp, 8, 128))
+    code = jnp.concatenate([code, code], axis=1).reshape(n_dp * SLEN, 128)
+    shape = (n_dp * SLEN, 128)
+    same = (iota(shape, 0) & 15) == (iota(shape, 1) & 15)
+    slot = ((iota(shape, 1) >> 4) + 1).astype(F32)
+    placer = jnp.where(same & (code == slot), 1.0, 0.0).astype(BF)
+    place_s[...] = placer
+    cbuf[...] = dot_nn(placer, scot[...]).astype(BF).reshape(cbuf.shape)
+    dp_start(cbuf, crecv, s_s, s_r)
+    crecv[dp] = cbuf[dp]
+
+    half_wait(down, 0, 0)
+    pass_copy(down, 0, up).start()
+    half_wait(up, 1, 1)
+    pass_copy(up, 1, down).start()
+    for d in (1, 3, 2):
+        c_copy(d).start()
 
     def wait_t(o, carry):
         src = lax.rem(ctx + 2 * CHIPS - o, 2 * CHIPS)
@@ -459,6 +465,55 @@
     dv_s[...] = jnp.zeros_like(dv_s)
     htot_s[...] = jnp.zeros_like(htot_s)
     tot_s[...] = jnp.zeros_like(tot_s)
+    mixed_s[...] = jnp.zeros_like(mixed_s)
+
+    half_wait(down, 1, 0)
+    project(down)
+    half_wait(up, 0, 1)
+    project(up)
+
+    table = jnp.broadcast_to(tab_s[pl.ds(chip, 1), :], (ROWS, 128))
+    length = llen[0]
+
+    def key_times(p):
+        return jnp.concatenate(
+            [times[2 * p, 0:1, :], times[2 * p + 1, 0:1, :]], axis=1
+        ).astype(F32)
+
+    def forward_tile(qs, p):
+        block = 2 * qs + core
+        queries = act_s[qs, :, 2 * HEAD : 3 * HEAD]
+        tq = tcol_s[block][:, 0:1]
+        spot = iota((ROWS, 1), 0) + block * ROWS
+        limit = jnp.where(spot < length, spot, -1)
+        keys = kv[rows_at(p, PAIR), 0:HEAD]
+        values = kv[rows_at(p, PAIR), HEAD : 2 * HEAD]
+        total = dot_nt(queries, keys) * SCALE + lookup(table, tq - key_times(p))
+        sg = sigmoid(total)
+        weight = total * sg
+        visible = (iota((ROWS, PAIR), 1) + p * PAIR) <= limit
+        weight16 = jnp.where(visible, weight, 0.0).astype(BF)
+        weight_s[qs, p] = weight16
+        slope_s[qs, p] = jnp.where(visible, sg + weight * (1.0 - sg), 0.0)
+        mixed_s[qs] += dot_nn(weight16, values)
+
+    for d in (0, 1, 3):
+        kv_wait(lax.rem(chip + CHIPS - d, CHIPS))
+
+    def near_block(step, carry):
+        qs = CHIPS - 1 - step
+
+        def one(p, carry):
+            @pl.when(p != far)
+            def _():
+                forward_tile(qs, p)
+
+            return carry
+
+        lax.fori_loop(0, jnp.where(qs == far, 0, qs + 1), one, 0)
+        return carry
+
+    lax.fori_loop(0, CHIPS, near_block, 0)
 
     for half in range(2):
         here = tok_all.at[rows_at(2 * far + half, half_rows), :]
@@ -469,11 +524,7 @@
     for d in (1, 3, 2):
         src = lax.rem(chip + CHIPS - d, CHIPS)
         remote(c_g.at[src], c_g.at[src], c_s.at[d], c_r.at[d], dp, sib).wait_recv()
-    for src in range(CHIPS):
-        kv_wait(src)
-
-    table = jnp.broadcast_to(tab_s[pl.ds(chip, 1), :], (ROWS, 128))
-    length = llen[0]
+    kv_wait(far)
 
     def stat_copy(qs, d):
         here = stat_s.at[qs, chip]
@@ -486,34 +537,16 @@
             2 * lax.rem(chip + d, CHIPS) + core,
         )
 
-    def key_times(p):
-        return jnp.concatenate(
-            [times[2 * p, 0:1, :], times[2 * p + 1, 0:1, :]], axis=1
-        ).astype(F32)
-
-    def forward(step, carry):
+    def far_block(step, carry):
         qs = CHIPS - 1 - step
-        block = 2 * qs + core
-        queries = act_s[qs, :, 2 * HEAD : 3 * HEAD]
-        tq = tcol_s[block][:, 0:1]
-        spot = iota((ROWS, 1), 0) + block * ROWS
-        limit = jnp.where(spot < length, spot, -1)
-        mixed_s[qs] = jnp.zeros((ROWS, HEAD), F32)
-
-        def tile(p, carry):
-            keys = kv[rows_at(p, PAIR), 0:HEAD]
-            values = kv[rows_at(p, PAIR), HEAD : 2 * HEAD]
-            total = dot_nt(queries, keys) * SCALE + lookup(table, tq - key_times(p))
-            sg = sigmoid(total)
-            weight = total * sg
-            visible = (iota((ROWS, PAIR), 1) + p * PAIR) <= limit
-            weight16 = jnp.where(visible, weight, 0.0).astype(BF)
-            weight_s[qs, p] = weight16
-            slope_s[qs, p] = jnp.where(visible, sg + weight * (1.0 - sg), 0.0)
-            mixed_s[qs] += dot_nn(weight16, values)
+
+        def one(p, carry):
+            forward_tile(qs, p)
             return carry
 
-        lax.fori_loop(0, qs + 1, tile, 0)
+        first = jnp.where(qs == far, 0, far)
+        last = jnp.where(qs >= far, jnp.where(qs == far, qs, far) + 1, first)
+        lax.fori_loop(first, last, one, 0)
         mixed = mixed_s[qs]
         q = c_g[qs].astype(F32) * act_s[qs, :, 0:HEAD].astype(F32)
         s1 = jnp.sum(mixed, axis=1, keepdims=True)
@@ -529,7 +562,7 @@
             stat_copy(qs, d).start()
         return carry
 
-    lax.fori_loop(0, CHIPS, forward, 0)
+    lax.fori_loop(0, CHIPS, far_block, 0)
 
     dp_all(cbuf, crecv, s_s, s_r).wait_recv()
     owner = jnp.concatenate([column_of(owner_row)] * (n_dp * SLEN // 128), axis=1)
@@ -578,7 +611,7 @@
         ]
         for k in range(4):
             lanes = slice(k * HEAD, (k + 1) * HEAD)
-            sgrad_s[h, :, lanes] = (grads[k] * silu_grad(sp_s[h, :, lanes])).astype(BF)
+            sgrad_s[h, :, lanes] = (grads[k] * sp_s[h, :, lanes]).astype(BF)
     sbias_s[...] = sums
     shape = (n_dp * SLEN, SHORT)
     same = (iota(shape, 0) & 15) == (iota(shape, 1) & 15)
@@ -609,7 +642,7 @@
 
     def l_copy(qs):
         return remote(
-            out_s.at[qs], long_out.at[:, lanes_at(chip)], l_s.at[qs], l_r.at[chip], dp, 2 * qs + core
+            out_s.at[qs], lo_v.at[:, lanes_at(chip)], l_s.at[qs], l_r.at[chip], dp, 2 * qs + core
         )
 
     def backward(step, carry):
@@ -638,7 +671,7 @@
         cotangent = c_g[qs].astype(F32)
         out_s[qs] = (normed * gates).astype(BF)
         mixed_grad = ((cotangent * gates - mean_q - normed * mean_qn) * scale).astype(BF)
-        grad_all[mine, 0:HEAD] = (cotangent * normed * silu_grad(p_s[qs, :, 0:HEAD])).astype(BF)
+        grad_all[mine, 0:HEAD] = (cotangent * normed * p_s[qs, :, 0:HEAD]).astype(BF)
 
         @pl.when(qs != chip)
         def _():
@@ -665,15 +698,12 @@
             return carry
 
         lax.fori_loop(0, qs + 1, tile, 0)
-        htot_s[...] += lax.dot_general(
-            hot_s[rows_at(block, ROWS), :].astype(F32),
-            hist_s[...],
-            (((0,), (0,)), ((), ())),
-            precision=lax.Precision.HIGHEST,
-            preferred_element_type=F32,
-        )
+        hot = hot_s[rows_at(block, ROWS), :]
+        high = hist_s[...].astype(BF)
+        low = (hist_s[...] - high.astype(F32)).astype(BF)
+        htot_s[...] += dot_tn(hot, high) + dot_tn(hot, low)
         grad_all[mine, 2 * HEAD : 3 * HEAD] = (
-            dq_s[...] * SCALE * silu_grad(p_s[qs, :, 2 * HEAD : 3 * HEAD])
+            dq_s[...] * SCALE * p_s[qs, :, 2 * HEAD : 3 * HEAD]
         ).astype(BF)
         other = rows_at(2 * qs + 1 - core, ROWS)
         sib_send[qs, :, 0:HEAD] = dk_s[other, :].astype(BF)
@@ -687,48 +717,6 @@
         return carry
 
     lax.fori_loop(0, CHIPS, backward, 0)
-
-    def finish(step, carry):
-        qs = CHIPS - 1 - step
-        sib_copy(qs).wait_recv()
-        mine = rows_at(qs, ROWS)
-        block = rows_at(2 * qs + core, ROWS)
-        dk = (dk_s[block, :] + sib_recv[qs, :, 0:HEAD].astype(F32)) * SCALE
-        dv = dv_s[block, :] + sib_recv[qs, :, HEAD : 2 * HEAD].astype(F32)
-        grad_all[mine, HEAD : 2 * HEAD] = (
-            dv * silu_grad(p_s[qs, :, HEAD : 2 * HEAD])
-        ).astype(BF)
-        grad_all[mine, 3 * HEAD : 4 * HEAD] = (
-            dk * silu_grad(p_s[qs, :, 3 * HEAD : 4 * HEAD])
-        ).astype(BF)
-
-        @pl.when(qs != chip)
-        def _():
-            g_copy(1, qs).start()
-            g_copy(3, qs).start()
-
-        return carry
-
-    lax.fori_loop(0, CHIPS, finish, 0)
-
-    for d in (1, 3, 2):
-        src = lax.rem(chip + CHIPS - d, CHIPS)
-        there = pl.ds(pl.multiple_of(LONG_ROWS + src * SHORT, SHORT), SHORT)
-        remote(stok, tok_all.at[there, :], st_s.at[d], st_r.at[d], dp, sib).wait_recv()
-        remote(sgrad_s.at[src], grad_all.at[there, :], sg_s.at[d], sg_r.at[d], dp, sib).wait_recv()
-
-    def outer(pair):
-        cols = pl.ds(pl.multiple_of(pair * 2 * HEAD, 2 * HEAD), 2 * HEAD)
-        return dot_tn(tok_all[...], grad_all[:, cols])
-
-    half_send[...] = outer(1 - core).astype(BF)
-    swap = remote(half_send, half_recv, p_ss, p_sr, dp, sib)
-    swap.start()
-    own[...] = outer(core)
-    swap.wait_recv()
-    rs_send[...] = (own[...] + half_recv[...].astype(F32)).astype(BF).reshape(rs_send.shape)
-    dp_start(rs_send, rs_recv, rs_s, rs_r)
-    rs_recv[dp] = rs_send[dp]
 
     shape = (128, 128)
     gap = (iota(shape, 0) - iota(shape, 1)) & 15
@@ -743,32 +731,102 @@
     levels = sbias_s[...] + jnp.where(level_lane == chip, levels, 0.0)
     levels = jnp.concatenate([levels, jnp.zeros((128 - LEVELS, 128), F32)], axis=0)
     b_send[...] = jnp.transpose(levels)[0:8, :]
-    one_start(b_send, b_dp, b1_s, b1_r)
-    b_dp[dp] = b_send[...]
+
+    def b2_copy(o):
+        return remote(
+            b_send, b_ctx.at[ctx], b2_s.at[o], b2_r.at[o], dp, lax.rem(ctx + o, 2 * CHIPS)
+        )
+
+    def start_b2(o, carry):
+        b2_copy(o).start()
+        return carry
+
+    lax.fori_loop(1, 2 * CHIPS, start_b2, 0)
+    b_ctx[ctx] = b_send[...]
+
+    def finish(step, carry):
+        qs = CHIPS - 1 - step
+        sib_copy(qs).wait_recv()
+        mine = rows_at(qs, ROWS)
+        block = rows_at(2 * qs + core, ROWS)
+        dk = (dk_s[block, :] + sib_recv[qs, :, 0:HEAD].astype(F32)) * SCALE
+        dv = dv_s[block, :] + sib_recv[qs, :, HEAD : 2 * HEAD].astype(F32)
+        grad_all[mine, HEAD : 2 * HEAD] = (
+            dv * p_s[qs, :, HEAD : 2 * HEAD]
+        ).astype(BF)
+        grad_all[mine, 3 * HEAD : 4 * HEAD] = (
+            dk * p_s[qs, :, 3 * HEAD : 4 * HEAD]
+        ).astype(BF)
+
+        @pl.when(qs != chip)
+        def _():
+            g_copy(1, qs).start()
+            g_copy(3, qs).start()
+
+        return carry
+
+    lax.fori_loop(0, CHIPS, finish, 0)
+
+    for d in (1, 3, 2):
+        src = lax.rem(chip + CHIPS - d, CHIPS)
+        there = pl.ds(pl.multiple_of(LONG_ROWS + src * SHORT, SHORT), SHORT)
+        remote(stok, tok_all.at[there, :], st_s.at[d], st_r.at[d], dp, sib).wait_recv()
+        remote(sgrad_s.at[src], grad_all.at[there, :], sg_s.at[d], sg_r.at[d], dp, sib).wait_recv()
+
+    half_dp = n_dp // 2
+    half_model = MODEL // 2
+    my_half = lax.div(dp, half_dp)
+    halves = (my_half, 1 - my_half)
+
+    def outer(pair, half):
+        cols = pl.ds(pl.multiple_of(pair * 2 * HEAD, 2 * HEAD), 2 * HEAD)
+        rows = pl.ds(pl.multiple_of(half * half_model, half_model), half_model)
+        return dot_tn(tok_all[:, rows], grad_all[:, cols])
+
+    def swap(j):
+        return remote(half_send.at[j], half_recv.at[j], p_ss.at[j], p_sr.at[j], dp, sib)
+
+    for j in range(2):
+        half_send[j] = outer(1 - core, halves[j]).astype(BF)
+        swap(j).start()
+    for j in range(2):
+        own[...] = outer(core, halves[j])
+        swap(j).wait_recv()
+        total = (own[...] + half_recv[j].astype(F32)).astype(BF)
+        first = halves[j] * half_dp
+        rs_send[pl.ds(first, half_dp)] = total.reshape((half_dp,) + rs_send.shape[1:])
+
+        def start_rs(o, carry):
+            peer = first + lax.rem(dp + o, half_dp)
+            remote(rs_send.at[peer], rs_recv.at[dp], rs_s, rs_r, peer, ctx).start()
+            return carry
+
+        lax.fori_loop(1 - j, half_dp, start_rs, 0)
+    rs_recv[dp] = rs_send[dp]
+
+    def wait_b2(o, carry):
+        src = lax.rem(ctx + 2 * CHIPS - o, 2 * CHIPS)
+        remote(b_send, b_ctx.at[src], b2_s.at[o], b2_r.at[o], dp, src).wait_recv()
+        return carry
+
+    lax.fori_loop(1, 2 * CHIPS, wait_b2, 0)
+    b_mid[...] = jnp.sum(b_ctx[...], axis=0)
+    one_start(b_mid, b_dp, b1_s, b1_r)
+    b_dp[dp] = b_mid[...]
+
+    def write(source, target, index):
+        return pltpu.make_async_copy(source, target, out_sem.at[index])
 
     dp_all(obuf, orecv, o_s, o_r).wait_recv()
-    short_out[...] = dot_tn(place_s[...], orecv[...].reshape(n_dp * SLEN, BLOCK)).astype(BF)
+    so_v[...] = dot_tn(place_s[...], orecv[...].reshape(n_dp * SLEN, BLOCK)).astype(BF)
+    write(so_v, short_out, 1).start()
     total = dot_nt(sgrad_s[0], wh[0])
     for h in range(1, 4):
         total = total + dot_nt(sgrad_s[h], wh[h])
-    short_grad[...] = total.astype(BF)
-
-    one_all(b_dp, b1_s, b1_r).wait_recv()
-    b_mid[...] = jnp.sum(b_dp[...], axis=0)
-
-    def b2_copy(o):
-        return remote(
-            b_mid, b_ctx.at[ctx], b2_s.at[o], b2_r.at[o], dp, lax.rem(ctx + o, 2 * CHIPS)
-        )
-
-    def start_b2(o, carry):
-        b2_copy(o).start()
-        return carry
-
-    lax.fori_loop(1, 2 * CHIPS, start_b2, 0)
-    b_ctx[ctx] = b_mid[...]
-
-    long_out[:, lanes_at(chip)] = out_s[chip]
+    sg_v[...] = total.astype(BF)
+    write(sg_v, short_grad, 3).start()
+
+    lo_v[:, lanes_at(chip)] = out_s[chip]
     grad_h[chip] = grad_all[rows_at(chip, ROWS), :]
     total = dot_nt(grad_h[chip], wh[chip])
     for d in (1, 3, 2):
@@ -776,18 +834,12 @@
         for k in range(4):
             here = grad_h.at[src, :, k * HEAD : (k + 1) * HEAD]
             remote(here, here, g_s.at[k, src], g_r.at[k, src], dp, sib).wait_recv()
-        here = long_out.at[:, lanes_at(src)]
+        here = lo_v.at[:, lanes_at(src)]
         remote(out_s.at[src], here, l_s.at[src], l_r.at[src], dp, sib).wait_recv()
         total = total + dot_nt(grad_h[src], wh[src])
-    token_grad[...] = total.astype(BF)
-
-    def wait_b2(o, carry):
-        src = lax.rem(ctx + 2 * CHIPS - o, 2 * CHIPS)
-        remote(b_mid, b_ctx.at[src], b2_s.at[o], b2_r.at[o], dp, src).wait_recv()
-        return carry
-
-    lax.fori_loop(1, 2 * CHIPS, wait_b2, 0)
-    bias_out[...] = jnp.sum(b_ctx[...], axis=0)[0:4, 0:LEVELS]
+    tg_v[...] = total.astype(BF)
+    write(tg_v, token_grad, 2).start()
+    write(lo_v, long_out, 0).start()
 
     half_copy(up, 0, 0).wait_send()
     half_copy(up, 1, 0).wait_send()
@@ -802,7 +854,6 @@
     one_all(dest_g, d_s, d_r).wait_send()
     dp_all(cbuf, crecv, s_s, s_r).wait_send()
     dp_all(obuf, orecv, o_s, o_r).wait_send()
-    one_all(b_dp, b1_s, b1_r).wait_send()
 
     def ended_o(o, carry):
         t_copy(o).wait_send()
@@ -826,7 +877,8 @@
         return carry
 
     lax.fori_loop(0, CHIPS, ended_q, 0)
-    swap.wait_send()
+    for j in range(2):
+        swap(j).wait_send()
 
     dp_all(rs_send, rs_recv, rs_s, rs_r).wait_recv()
     piece[...] = jnp.sum(rs_recv[...].astype(F32), axis=0)
@@ -853,6 +905,9 @@
         @pl.when(target == ctx)
         def _():
             proj_grad[:, lanes_at(mine)] = piece[:, i * HEAD : (i + 1) * HEAD]
+
+    one_all(b_dp, b1_s, b1_r).wait_recv()
+    bias_out[...] = jnp.sum(b_dp[...], axis=0)[0:4, 0:LEVELS]
 
     for half in range(2):
         source = 2 * (2 * core + half) + lax.div(chip, 2)
@@ -876,6 +931,11 @@
             copy.wait_send()
 
     dp_all(rs_send, rs_recv, rs_s, rs_r).wait_send()
+    one_all(b_dp, b1_s, b1_r).wait_send()
+    write(lo_v, long_out, 0).wait()
+    write(so_v, short_out, 1).wait()
+    write(tg_v, token_grad, 2).wait()
+    write(sg_v, short_grad, 3).wait()
 
 
 def output_kernel(count, *refs):
@@ -954,9 +1014,9 @@
         VMEM((CHIPS, ROWS, 2 * HEAD), BF),
         VMEM((CHIPS, ROWS, 2 * HEAD), BF),
         VMEM((CHIPS, ROWS, BLOCK), BF),
-        VMEM((MODEL, 2 * HEAD), BF),
-        VMEM((MODEL, 2 * HEAD), BF),
-        VMEM((MODEL, 2 * HEAD), F32),
+        VMEM((2, MODEL // 2, 2 * HEAD), BF),
+        VMEM((2, MODEL // 2, 2 * HEAD), BF),
+        VMEM((MODEL // 2, 2 * HEAD), F32),
         VMEM((n_dp, part, 2 * HEAD), BF),
         VMEM((n_dp, part, 2 * HEAD), BF),
         VMEM((8, 128), F32),
@@ -964,7 +1024,13 @@
         VMEM((8, 128), F32),
         VMEM((2 * CHIPS, 8, 128), F32),
         VMEM((part, 2 * HEAD), F32),
+        VMEM((ROWS, BLOCK), BF),
+        VMEM((SHORT, BLOCK), BF),
+        VMEM((ROWS, MODEL), BF),
+        VMEM((SHORT, MODEL), BF),
         DMA((4, 4)),
+        DMA((3,)),
+        DMA((4,)),
         DMA((2, 2)),
         DMA((2, 2)),
         DMA((2,)),
@@ -993,8 +1059,8 @@
         DMA((4, CHIPS)),
         DMA((CHIPS,)),
         DMA((CHIPS,)),
-        DMA,
-        DMA,
+        DMA((2,)),
+        DMA((2,)),
         DMA,
         DMA,
         DMA,
@@ -1014,8 +1080,8 @@
             shaped((part, 2 * HEAD), F32),
             shaped(time_bias.shape, F32),
         ),
-        in_specs=[VM, VM, ANY, VM, VM, VM, VM, VM, VM, SM, VM],
-        out_specs=(VM,) * 6,
+        in_specs=[ANY, ANY, ANY, ANY, VM, VM, VM, VM, VM, SM, VM],
+        out_specs=(ANY,) * 4 + (VM,) * 2,
         scratch_shapes=scratch,
         compiler_params=pltpu.CompilerParams(
             vmem_limit_bytes=VMEM_LIMIT, collective_id=0, has_side_effects=True

time: 93.4 us -> 89.3 us (0.956)
  Pallas kernels: 92 us -> 87.9 us
    pallas_call x1, Pallas kernels: 89.7 us -> 85.6 us  [per_device(): pl.pallas_call(functools.partial(layer_kernel, n_dp), out_shape=(shaped((...]
where the time goes in v3:
time: 89.3 us; the launch traced here: 89.2 us
  Pallas kernels  87.9 us (98%)
  between operations  1.29 us (1%)
    pallas_call x1, Pallas kernels, per_device(): pl.pallas_call(functools.partial(layer_kernel, n_dp), out_shape=(shaped((...  85.6 us
    pallas_call x1, Pallas kernels, per_device(): pl.pallas_call(functools.partial(output_kernel, len(results)), out_shape=...  2.3 us

profile of v3, /device:TPU:1, one launch (start us, length us, event | category | flops | bytes accessed | tf_op | source)
XLA Modules:
  0.0 89.2 jit_solution(7509644538306327268)
XLA Ops:
  1.3 85.6 %layer.1 = (bf16[256,512]{1,0:T(8,128)(2,1)}, bf16[128,512]{1,0:T(8,128)(2,1)}, bf16[256,1024]{1,0:T(8,128)(2,1)}, bf16[128,1024]{1,0:T(8,128)(2,1)}, f32[32,256]{1,0:T(8,128)}, /*index=5*/f32[4,16]{1,0:T(4,128)}) custom-call(bf16[256,1024]{1,0:T(8,128)(2,1)} %bitcast.8, bf16[128,1024]{1,0:T(8,128)(2,1)} %bitcast.9, bf16[1024,2048]{1,0:T(8,128)(2,1)} %w.1, ...), custom_call_target="tpu_custom_call" | custom-call | tf_op jit(solution)/shard_map/layer/pallas_call | solution.py:1073
  86.9 2.3 %output.1 = (bf16[256,512]{1,0:T(8,128)(2,1)}, bf16[128,512]{1,0:T(8,128)(2,1)}, bf16[256,1024]{1,0:T(8,128)(2,1)}, bf16[128,1024]{1,0:T(8,128)(2,1)}, f32[32,256]{1,0:T(8,128)}, /*index=5*/f32[4,16]{1,0:T(4,128)}) custom-call(bf16[256,512]{1,0:T(8,128)(2,1)} %get-tuple-element.18.refs_0_, bf16[128,512]{1,0:T(8,128)(2,1)} %get-tuple-element.19.refs_1_, ...), custom_call_target="tpu_custom_call" | custom-call | tf_op jit(solution)/shard_map/output/pallas_call | solution.py:1103

commit v4 on v3

--- a/solution.py
+++ b/solution.py
@@ -12,6 +12,7 @@
 BF = jnp.bfloat16
 F32 = jnp.float32
 CHIPS = 4
+NZ = 8
 ROWS = 256
 HEAD = 128
 LEVELS = 16
@@ -144,6 +145,7 @@
     c_home,
     sgrad_s,
     obuf,
+    omid,
     orecv,
     sbias_s,
     weight_s,
@@ -166,7 +168,9 @@
     half_recv,
     own,
     rs_send,
-    rs_recv,
+    rs_mid,
+    rs_sum,
+    rs_fin,
     b_send,
     b_dp,
     b_mid,
@@ -197,8 +201,10 @@
     d_r,
     s_s,
     s_r,
-    o_s,
-    o_r,
+    oy_s,
+    oy_r,
+    oz_s,
+    oz_r,
     stat_ss,
     stat_sr,
     sib_s,
@@ -209,8 +215,10 @@
     l_r,
     p_ss,
     p_sr,
-    rs_s,
-    rs_r,
+    ry_s,
+    ry_r,
+    rz_s,
+    rz_r,
     b1_s,
     b1_r,
     b2_s,
@@ -224,6 +232,8 @@
     down = lax.rem(chip + CHIPS - 1, CHIPS)
     far = lax.rem(chip + 2, CHIPS)
     half_rows = ROWS // 2
+    ny = n_dp // NZ
+    y, z = lax.div(dp, NZ), lax.rem(dp, NZ)
     barrier = pltpu.get_barrier_semaphore()
 
     def greet_ctx(o, carry):
@@ -622,8 +632,22 @@
     for d in (1, 3, 2):
         sg_copy(d).start()
     grad_all[pl.ds(pl.multiple_of(LONG_ROWS + chip * SHORT, SHORT), SHORT), :] = sgrad_s[chip]
-    dp_start(obuf, orecv, o_s, o_r)
-    orecv[dp] = obuf[dp]
+
+    def oy_copy(o):
+        peer = lax.rem(y + o, ny)
+        return remote(
+            obuf.at[peer], omid.at[y], oy_s.at[o], oy_r.at[o], peer * NZ + z, ctx
+        )
+
+    def oz_copy(o):
+        peer = lax.rem(z + o, NZ)
+        return remote(
+            omid.at[:, peer], orecv.at[:, z], oz_s.at[o], oz_r.at[o], y * NZ + peer, ctx
+        )
+
+    for o in range(1, ny):
+        oy_copy(o).start()
+    omid[y] = obuf[y]
 
     def sib_copy(qs):
         return remote(
@@ -718,6 +742,13 @@
 
     lax.fori_loop(0, CHIPS, backward, 0)
 
+    for o in range(1, ny):
+        here = omid.at[lax.rem(y + ny - o, ny)]
+        remote(here, here, oy_s.at[o], oy_r.at[o], dp, sib).wait_recv()
+    for o in range(1, NZ):
+        oz_copy(o).start()
+    orecv[:, z] = omid[:, z]
+
     shape = (128, 128)
     gap = (iota(shape, 0) - iota(shape, 1)) & 15
     hist = htot_s[...]
@@ -786,6 +817,17 @@
     def swap(j):
         return remote(half_send.at[j], half_recv.at[j], p_ss.at[j], p_sr.at[j], dp, sib)
 
+    def ry_copy(o):
+        return remote(
+            rs_send.at[y ^ o], rs_mid.at[y], ry_s.at[o], ry_r.at[o], (y ^ o) * NZ + z, ctx
+        )
+
+    def rz_copy(o):
+        peer = lax.rem(z + o, NZ)
+        return remote(
+            rs_sum.at[peer], rs_fin.at[z], rz_s.at[o], rz_r.at[o], y * NZ + peer, ctx
+        )
+
     for j in range(2):
         half_send[j] = outer(1 - core, halves[j]).astype(BF)
         swap(j).start()
@@ -793,16 +835,11 @@
         own[...] = outer(core, halves[j])
         swap(j).wait_recv()
         total = (own[...] + half_recv[j].astype(F32)).astype(BF)
-        first = halves[j] * half_dp
-        rs_send[pl.ds(first, half_dp)] = total.reshape((half_dp,) + rs_send.shape[1:])
-
-        def start_rs(o, carry):
-            peer = first + lax.rem(dp + o, half_dp)
-            remote(rs_send.at[peer], rs_recv.at[dp], rs_s, rs_r, peer, ctx).start()
-            return carry
-
-        lax.fori_loop(1 - j, half_dp, start_rs, 0)
-    rs_recv[dp] = rs_send[dp]
+        rs_send[pl.ds(halves[j] * (ny // 2), ny // 2)] = total.reshape(
+            (ny // 2,) + rs_send.shape[1:]
+        )
+        for o in ((1,), (2, 3))[j]:
+            ry_copy(o).start()
 
     def wait_b2(o, carry):
         src = lax.rem(ctx + 2 * CHIPS - o, 2 * CHIPS)
@@ -817,7 +854,9 @@
     def write(source, target, index):
         return pltpu.make_async_copy(source, target, out_sem.at[index])
 
-    dp_all(obuf, orecv, o_s, o_r).wait_recv()
+    for o in range(1, NZ):
+        here = orecv.at[:, lax.rem(z + NZ - o, NZ)]
+        remote(here, here, oz_s.at[o], oz_r.at[o], dp, sib).wait_recv()
     so_v[...] = dot_tn(place_s[...], orecv[...].reshape(n_dp * SLEN, BLOCK)).astype(BF)
     write(so_v, short_out, 1).start()
     total = dot_nt(sgrad_s[0], wh[0])
@@ -825,6 +864,15 @@
         total = total + dot_nt(sgrad_s[h], wh[h])
     sg_v[...] = total.astype(BF)
     write(sg_v, short_grad, 3).start()
+
+    total = rs_send[y].astype(F32)
+    for o in range(1, ny):
+        here = rs_mid.at[y ^ o]
+        remote(here, here, ry_s.at[o], ry_r.at[o], dp, sib).wait_recv()
+        total = total + rs_mid[y ^ o].astype(F32)
+    rs_sum[...] = total.astype(BF)
+    for o in range(1, NZ):
+        rz_copy(o).start()
 
     lo_v[:, lanes_at(chip)] = out_s[chip]
     grad_h[chip] = grad_all[rows_at(chip, ROWS), :]
@@ -853,7 +901,11 @@
         sg_copy(d).wait_send()
     one_all(dest_g, d_s, d_r).wait_send()
     dp_all(cbuf, crecv, s_s, s_r).wait_send()
-    dp_all(obuf, orecv, o_s, o_r).wait_send()
+    for o in range(1, ny):
+        oy_copy(o).wait_send()
+        ry_copy(o).wait_send()
+    for o in range(1, NZ):
+        oz_copy(o).wait_send()
 
     def ended_o(o, carry):
         t_copy(o).wait_send()
@@ -880,8 +932,13 @@
     for j in range(2):
         swap(j).wait_send()
 
-    dp_all(rs_send, rs_recv, rs_s, rs_r).wait_recv()
-    piece[...] = jnp.sum(rs_recv[...].astype(F32), axis=0)
+    total = rs_sum[z].astype(F32)
+    for o in range(1, NZ):
+        src = lax.rem(z + NZ - o, NZ)
+        here = rs_fin.at[src]
+        remote(here, here, rz_s.at[o], rz_r.at[o], dp, sib).wait_recv()
+        total = total + rs_fin[src].astype(F32)
+    piece[...] = total
     mine = lax.rem(chip, 2)
 
     def f_copy(i):
@@ -930,7 +987,8 @@
         def _():
             copy.wait_send()
 
-    dp_all(rs_send, rs_recv, rs_s, rs_r).wait_send()
+    for o in range(1, NZ):
+        rz_copy(o).wait_send()
     one_all(b_dp, b1_s, b1_r).wait_send()
     write(lo_v, long_out, 0).wait()
     write(so_v, short_out, 1).wait()
@@ -969,6 +1027,7 @@
     short_cotangent,
 ):
     part = MODEL // n_dp
+    ny = n_dp // NZ
     spread = (n_dp, SLEN, BLOCK)
     scratch = [
         VMEM((CHIPS, MODEL, BLOCK), BF),
@@ -995,8 +1054,9 @@
         VMEM((SHORT, 128), F32),
         VMEM((SHORT, BLOCK), F32),
         VMEM((4, SHORT, BLOCK), BF),
-        VMEM(spread, BF),
-        VMEM(spread, BF),
+        VMEM((ny, NZ, SLEN, BLOCK), BF),
+        VMEM((ny, NZ, SLEN, BLOCK), BF),
+        VMEM((ny, NZ, SLEN, BLOCK), BF),
         VMEM((LEVELS, 128), F32),
         VMEM((CHIPS, CHIPS, ROWS, PAIR), BF),
         VMEM((CHIPS, CHIPS, ROWS, PAIR), F32),
@@ -1017,8 +1077,10 @@
         VMEM((2, MODEL // 2, 2 * HEAD), BF),
         VMEM((2, MODEL // 2, 2 * HEAD), BF),
         VMEM((MODEL // 2, 2 * HEAD), F32),
-        VMEM((n_dp, part, 2 * HEAD), BF),
-        VMEM((n_dp, part, 2 * HEAD), BF),
+        VMEM((ny, NZ, part, 2 * HEAD), BF),
+        VMEM((ny, NZ, part, 2 * HEAD), BF),
+        VMEM((NZ, part, 2 * HEAD), BF),
+        VMEM((NZ, part, 2 * HEAD), BF),
         VMEM((8, 128), F32),
         VMEM((n_dp, 8, 128), F32),
         VMEM((8, 128), F32),
@@ -1049,8 +1111,10 @@
         DMA,
         DMA,
         DMA,
-        DMA,
-        DMA,
+        DMA((ny,)),
+        DMA((ny,)),
+        DMA((NZ,)),
+        DMA((NZ,)),
         DMA((CHIPS, CHIPS)),
         DMA((CHIPS, CHIPS)),
         DMA((CHIPS,)),
@@ -1061,8 +1125,10 @@
         DMA((CHIPS,)),
         DMA((2,)),
         DMA((2,)),
-        DMA,
-        DMA,
+        DMA((ny,)),
+        DMA((ny,)),
+        DMA((NZ,)),
+        DMA((NZ,)),
         DMA,
         DMA,
         DMA((2 * CHIPS,)),

time: 89.3 us -> 92.2 us (1.032)
  Pallas kernels: 87.9 us -> 90.8 us
    pallas_call x1, Pallas kernels: 85.6 us -> 88.5 us  [per_device(): pl.pallas_call(functools.partial(layer_kernel, n_dp), out_shape=(shaped((...]
where the time goes in v4:
time: 92.2 us; the launch traced here: 92 us
  Pallas kernels  90.8 us (98%)
  between operations  1.29 us (1%)
    pallas_call x1, Pallas kernels, per_device(): pl.pallas_call(functools.partial(layer_kernel, n_dp), out_shape=(shaped((...  88.5 us
    pallas_call x1, Pallas kernels, per_device(): pl.pallas_call(functools.partial(output_kernel, len(results)), out_shape=...  2.3 us

profile of v4, /device:TPU:1, one launch (start us, length us, event | category | flops | bytes accessed | tf_op | source)
XLA Modules:
  0.0 92.0 jit_solution(14474956165517733874)
XLA Ops:
  1.3 88.5 %layer.1 = (bf16[256,512]{1,0:T(8,128)(2,1)}, bf16[128,512]{1,0:T(8,128)(2,1)}, bf16[256,1024]{1,0:T(8,128)(2,1)}, bf16[128,1024]{1,0:T(8,128)(2,1)}, f32[32,256]{1,0:T(8,128)}, /*index=5*/f32[4,16]{1,0:T(4,128)}) custom-call(bf16[256,1024]{1,0:T(8,128)(2,1)} %bitcast.8, bf16[128,1024]{1,0:T(8,128)(2,1)} %bitcast.9, bf16[1024,2048]{1,0:T(8,128)(2,1)} %w.1, ...), custom_call_target="tpu_custom_call" | custom-call | tf_op jit(solution)/shard_map/layer/pallas_call | solution.py:1139
  89.7 2.3 %output.1 = (bf16[256,512]{1,0:T(8,128)(2,1)}, bf16[128,512]{1,0:T(8,128)(2,1)}, bf16[256,1024]{1,0:T(8,128)(2,1)}, bf16[128,1024]{1,0:T(8,128)(2,1)}, f32[32,256]{1,0:T(8,128)}, /*index=5*/f32[4,16]{1,0:T(4,128)}) custom-call(bf16[256,512]{1,0:T(8,128)(2,1)} %get-tuple-element.18.refs_0_, bf16[128,512]{1,0:T(8,128)(2,1)} %get-tuple-element.19.refs_1_, ...), custom_call_target="tpu_custom_call" | custom-call | tf_op jit(solution)/shard_map/output/pallas_call | solution.py:1169

commit v5 on v4

--- a/solution.py
+++ b/solution.py
@@ -671,6 +671,16 @@
 
     def backward(step, carry):
         qs = CHIPS - 1 - step
+
+        @pl.when(step == CHIPS - 1)
+        def _():
+            for o in range(1, ny):
+                here = omid.at[lax.rem(y + ny - o, ny)]
+                remote(here, here, oy_s.at[o], oy_r.at[o], dp, sib).wait_recv()
+            for o in range(1, NZ):
+                oz_copy(o).start()
+            orecv[:, z] = omid[:, z]
+
         block = 2 * qs + core
         mine = rows_at(qs, ROWS)
         for d in (1, 3, 2):
@@ -742,13 +752,6 @@
 
     lax.fori_loop(0, CHIPS, backward, 0)
 
-    for o in range(1, ny):
-        here = omid.at[lax.rem(y + ny - o, ny)]
-        remote(here, here, oy_s.at[o], oy_r.at[o], dp, sib).wait_recv()
-    for o in range(1, NZ):
-        oz_copy(o).start()
-    orecv[:, z] = omid[:, z]
-
     shape = (128, 128)
     gap = (iota(shape, 0) - iota(shape, 1)) & 15
     hist = htot_s[...]
@@ -854,11 +857,6 @@
     def write(source, target, index):
         return pltpu.make_async_copy(source, target, out_sem.at[index])
 
-    for o in range(1, NZ):
-        here = orecv.at[:, lax.rem(z + NZ - o, NZ)]
-        remote(here, here, oz_s.at[o], oz_r.at[o], dp, sib).wait_recv()
-    so_v[...] = dot_tn(place_s[...], orecv[...].reshape(n_dp * SLEN, BLOCK)).astype(BF)
-    write(so_v, short_out, 1).start()
     total = dot_nt(sgrad_s[0], wh[0])
     for h in range(1, 4):
         total = total + dot_nt(sgrad_s[h], wh[h])
@@ -873,6 +871,12 @@
     rs_sum[...] = total.astype(BF)
     for o in range(1, NZ):
         rz_copy(o).start()
+
+    for o in range(1, NZ):
+        here = orecv.at[:, lax.rem(z + NZ - o, NZ)]
+        remote(here, here, oz_s.at[o], oz_r.at[o], dp, sib).wait_recv()
+    so_v[...] = dot_tn(place_s[...], orecv[...].reshape(n_dp * SLEN, BLOCK)).astype(BF)
+    write(so_v, short_out, 1).start()
 
     lo_v[:, lanes_at(chip)] = out_s[chip]
     grad_h[chip] = grad_all[rows_at(chip, ROWS), :]

time: 92.2 us -> 89.2 us (0.967)
  Pallas kernels: 90.8 us -> 87.7 us
    pallas_call x1, Pallas kernels: 88.5 us -> 85.4 us  [per_device(): pl.pallas_call(functools.partial(layer_kernel, n_dp), out_shape=(shaped((...]
where the time goes in v5:
time: 89.2 us; the launch traced here: 89 us
  Pallas kernels  87.7 us (98%)
  between operations  1.29 us (1%)
    pallas_call x1, Pallas kernels, per_device(): pl.pallas_call(functools.partial(layer_kernel, n_dp), out_shape=(shaped((...  85.4 us
    pallas_call x1, Pallas kernels, per_device(): pl.pallas_call(functools.partial(output_kernel, len(results)), out_shape=...  2.3 us

profile of v5, /device:TPU:1, one launch (start us, length us, event | category | flops | bytes accessed | tf_op | source)
XLA Modules:
  0.0 89.0 jit_solution(14702290950436348221)
XLA Ops:
  1.3 85.4 %layer.1 = (bf16[256,512]{1,0:T(8,128)(2,1)}, bf16[128,512]{1,0:T(8,128)(2,1)}, bf16[256,1024]{1,0:T(8,128)(2,1)}, bf16[128,1024]{1,0:T(8,128)(2,1)}, f32[32,256]{1,0:T(8,128)}, /*index=5*/f32[4,16]{1,0:T(4,128)}) custom-call(bf16[256,1024]{1,0:T(8,128)(2,1)} %bitcast.8, bf16[128,1024]{1,0:T(8,128)(2,1)} %bitcast.9, bf16[1024,2048]{1,0:T(8,128)(2,1)} %w.1, ...), custom_call_target="tpu_custom_call" | custom-call | tf_op jit(solution)/shard_map/layer/pallas_call | solution.py:1143
  86.7 2.3 %output.1 = (bf16[256,512]{1,0:T(8,128)(2,1)}, bf16[128,512]{1,0:T(8,128)(2,1)}, bf16[256,1024]{1,0:T(8,128)(2,1)}, bf16[128,1024]{1,0:T(8,128)(2,1)}, f32[32,256]{1,0:T(8,128)}, /*index=5*/f32[4,16]{1,0:T(4,128)}) custom-call(bf16[256,512]{1,0:T(8,128)(2,1)} %get-tuple-element.18.refs_0_, bf16[128,512]{1,0:T(8,128)(2,1)} %get-tuple-element.19.refs_1_, ...), custom_call_target="tpu_custom_call" | custom-call | tf_op jit(solution)/shard_map/output/pallas_call | solution.py:1173

commit v6 on v5

--- a/solution.py
+++ b/solution.py
@@ -810,7 +810,7 @@
     half_dp = n_dp // 2
     half_model = MODEL // 2
     my_half = lax.div(dp, half_dp)
-    halves = (my_half, 1 - my_half)
+    halves = (1 - my_half, my_half)
 
     def outer(pair, half):
         cols = pl.ds(pl.multiple_of(pair * 2 * HEAD, 2 * HEAD), 2 * HEAD)
@@ -841,7 +841,7 @@
         rs_send[pl.ds(halves[j] * (ny // 2), ny // 2)] = total.reshape(
             (ny // 2,) + rs_send.shape[1:]
         )
-        for o in ((1,), (2, 3))[j]:
+        for o in ((2, 3), (1,))[j]:
             ry_copy(o).start()
 
     def wait_b2(o, carry):
@@ -851,8 +851,6 @@
 
     lax.fori_loop(1, 2 * CHIPS, wait_b2, 0)
     b_mid[...] = jnp.sum(b_ctx[...], axis=0)
-    one_start(b_mid, b_dp, b1_s, b1_r)
-    b_dp[dp] = b_mid[...]
 
     def write(source, target, index):
         return pltpu.make_async_copy(source, target, out_sem.at[index])
@@ -871,6 +869,9 @@
     rs_sum[...] = total.astype(BF)
     for o in range(1, NZ):
         rz_copy(o).start()
+
+    one_start(b_mid, b_dp, b1_s, b1_r)
+    b_dp[dp] = b_mid[...]
 
     for o in range(1, NZ):
         here = orecv.at[:, lax.rem(z + NZ - o, NZ)]

time: 89.2 us -> 89.1 us (level)
  no operation moved by 1% of the time
where the time goes in v6:
time: 89.1 us; the launch traced here: 89 us
  Pallas kernels  87.7 us (98%)
  between operations  1.29 us (1%)
    pallas_call x1, Pallas kernels, per_device(): pl.pallas_call(functools.partial(layer_kernel, n_dp), out_shape=(shaped((...  85.4 us
    pallas_call x1, Pallas kernels, per_device(): pl.pallas_call(functools.partial(output_kernel, len(results)), out_shape=...  2.3 us

profile of v6, /device:TPU:1, one launch (start us, length us, event | category | flops | bytes accessed | tf_op | source)
XLA Modules:
  0.0 89.0 jit_solution(7412768302200342898)
XLA Ops:
  1.3 85.4 %layer.1 = (bf16[256,512]{1,0:T(8,128)(2,1)}, bf16[128,512]{1,0:T(8,128)(2,1)}, bf16[256,1024]{1,0:T(8,128)(2,1)}, bf16[128,1024]{1,0:T(8,128)(2,1)}, f32[32,256]{1,0:T(8,128)}, /*index=5*/f32[4,16]{1,0:T(4,128)}) custom-call(bf16[256,1024]{1,0:T(8,128)(2,1)} %bitcast.8, bf16[128,1024]{1,0:T(8,128)(2,1)} %bitcast.9, bf16[1024,2048]{1,0:T(8,128)(2,1)} %w.1, ...), custom_call_target="tpu_custom_call" | custom-call | tf_op jit(solution)/shard_map/layer/pallas_call | solution.py:1144
  86.7 2.3 %output.1 = (bf16[256,512]{1,0:T(8,128)(2,1)}, bf16[128,512]{1,0:T(8,128)(2,1)}, bf16[256,1024]{1,0:T(8,128)(2,1)}, bf16[128,1024]{1,0:T(8,128)(2,1)}, f32[32,256]{1,0:T(8,128)}, /*index=5*/f32[4,16]{1,0:T(4,128)}) custom-call(bf16[256,512]{1,0:T(8,128)(2,1)} %get-tuple-element.18.refs_0_, bf16[128,512]{1,0:T(8,128)(2,1)} %get-tuple-element.19.refs_1_, ...), custom_call_target="tpu_custom_call" | custom-call | tf_op jit(solution)/shard_map/output/pallas_call | solution.py:1174
